TPU v7x, 32 devices: a whole 2x2x4 slice. The times are simulated.
32 devices in a mesh: seq: 4 (over y, x), ctx: 8 (over z, core).
Axes of the slice: x: 2, y: 2, z: 4, core: 2. Of those that a mesh axis runs over, the one named last changes fastest.
Arguments:
- tokens: bfloat16 [8, 2048, 768], P('seq', 'ctx'), may hold values from -6 to 6
- norm_gain: float32 [768], replicated, may hold values from 0.5 to 1.5
- gate_projection_matrix: bfloat16 [768, 1536], replicated, may hold values from -0.21875 to 0.21875
- mixer_projection_matrix: bfloat16 [768, 1792], replicated, may hold values from -0.21875 to 0.21875
- step_projection_matrix: bfloat16 [768, 24], replicated, may hold values from -0.21875 to 0.21875
- conv_weight: float32 [4, 1792], replicated, may hold values from -3 to 3
- conv_bias: float32 [1792], replicated, may hold values from -3 to 3
- step_bias: float32 [24], replicated, may hold values from -2 to 0
- log_rates: float32 [24], replicated, may hold values from -12 to -2, as said below
- skip_gain: float32 [24], replicated, may hold values from 0.5 to 2
- gate_gain: float32 [1536], replicated, may hold values from 0.5 to 1.5
- out_weight: bfloat16 [1536, 768], replicated, may hold values from -0.15625 to 0.15625
- cotangent: bfloat16 [8, 2048, 768], P('seq', 'ctx'), may hold values from -6 to 6
Outputs:
- result: bfloat16 [8, 2048, 768], P('seq', 'ctx')
- token_grad: bfloat16 [8, 2048, 768], P('seq', 'ctx')
- grad_norm_gain: float32 [768], replicated
- grad_gate_weight: float32 [768, 1536], replicated
- grad_mixer_weight: float32 [768, 1792], replicated
- grad_step_weight: float32 [768, 24], replicated
- grad_conv_weight: float32 [4, 1792], replicated
- grad_conv_bias: float32 [1792], replicated
- grad_step_bias: float32 [24], replicated
- grad_log_rates: float32 [24], replicated
- grad_skip_gain: float32 [24], replicated
- grad_gate_gain: float32 [1536], replicated
- grad_out_weight: float32 [1536, 768], replicated
Inputs may be any that keep to these rules, and one draw needn't show every extreme that they name: `log_rates`: logarithms of the heads' decay rates.
All inputs are finite; a program needn't handle non-finite values.
Results may differ from a plain program's by a relative error of at most 0.0055.
The roundings to bfloat16 on the way count: a program that leaves them out, or rounds other values in their place, can miss the bound.
Values may be sent and summed in bfloat16 or wider, within the bound.
A program may use at most 256 MiB of HBM per device.

v0:
```python
import jax
import jax.numpy as jnp
from jax import lax
from jax.sharding import PartitionSpec as P

EPSILON = 1e-05
HIGHEST = lax.Precision.HIGHEST


def passed_along(block, axis, distance):
    devices = range(lax.axis_size(axis))
    route = [(i - distance, i) for i in devices if i - distance in devices]
    return lax.ppermute(block, axis, route)


def swish(value):
    return value * jax.nn.sigmoid(value)


def swish_grad(value):
    sigmoid_v = jax.nn.sigmoid(value)
    return sigmoid_v * (1.0 + value * (1.0 - sigmoid_v))


def heads_wide(value, head_size):
    return jnp.repeat(value, head_size, axis=-1)


def head_sums(value, head_count):
    return jnp.sum(value.reshape(value.shape[:-1] + (head_count, -1)), axis=-1)


def rms_back(grad_unit, unit_value, inverse):
    return inverse * (
        grad_unit - unit_value * jnp.mean(grad_unit * unit_value, axis=-1, keepdims=True)
    )


def on_device(
    tokens,
    norm_gain,
    gate_projection_matrix,
    mixer_projection_matrix,
    step_projection_matrix,
    conv_weight,
    conv_bias,
    step_bias,
    log_rates,
    skip_gain,
    gate_gain,
    out_weight,
    cotangent,
):
    seqs_here, length, model_width = tokens.shape
    inner_width = gate_projection_matrix.shape[1]
    head_count = step_projection_matrix.shape[1]
    head_size = inner_width // head_count
    state_width = (mixer_projection_matrix.shape[1] - inner_width) // 2
    window = conv_weight.shape[0] - 1
    hidden = tokens.astype(jnp.float32)
    inverse = lax.rsqrt(jnp.mean(hidden * hidden, axis=-1, keepdims=True) + EPSILON)
    unit_in = hidden * inverse
    normalized_input = (unit_in * norm_gain).astype(jnp.bfloat16)
    gate_preactivation = jnp.einsum(
        "bfu,un->bfn", normalized_input, gate_projection_matrix, preferred_element_type=jnp.float32
    )
    mixed = jnp.einsum(
        "bfu,un->bfn", normalized_input, mixer_projection_matrix, preferred_element_type=jnp.float32
    ).astype(jnp.bfloat16)
    step_preactivation = jnp.einsum(
        "bfu,un->bfn", normalized_input, step_projection_matrix, preferred_element_type=jnp.float32
    )
    previous = passed_along(mixed[:, length - window :, :], "ctx", 1)
    extended = jnp.concatenate([previous, mixed], axis=1).astype(jnp.float32)
    filtered = conv_bias
    for offset in range(window + 1):
        filtered = filtered + conv_weight[offset] * extended[:, offset : offset + length]
    activated = swish(filtered)
    signal = activated[..., :inner_width]
    inflow = activated[..., inner_width : inner_width + state_width].astype(jnp.bfloat16)
    outflow = activated[..., inner_width + state_width :].astype(jnp.bfloat16)
    inflow_wide = inflow.astype(jnp.float32)
    outflow_wide = outflow.astype(jnp.float32)
    step_size = jax.nn.softplus(step_preactivation + step_bias)
    rates = -jnp.exp(log_rates)
    cumulative = jnp.cumsum(step_size * rates, axis=1)
    block_decay = cumulative[:, -1, :]
    step_wide = heads_wide(step_size, head_size)
    tail = jnp.exp(block_decay[:, None, :] - cumulative)
    tail_wide = heads_wide(tail, head_size)
    driven = (signal * step_wide).astype(jnp.bfloat16)
    scaled = (signal * step_wide * tail_wide).astype(jnp.bfloat16)
    summary = jnp.einsum("slp,sln->spn", scaled, inflow, preferred_element_type=jnp.float32)
    scores = jnp.einsum("stn,sun->stu", outflow, inflow, preferred_element_type=jnp.float32)
    positions = jnp.arange(length)
    causal = positions[:, None] >= positions[None, :]
    by_head = cumulative.transpose(0, 2, 1)
    gaps = by_head[:, :, :, None] - by_head[:, :, None, :]
    factor = jnp.where(causal, jnp.exp(jnp.where(causal, gaps, 0.0)), 0.0)
    mixing = (scores[:, None] * factor).astype(jnp.bfloat16)
    driven_heads = driven.reshape(seqs_here, length, head_count, head_size)
    inner_part = jnp.einsum(
        "shtu,suhp->sthp", mixing, driven_heads, preferred_element_type=jnp.float32
    ).reshape(seqs_here, length, inner_width)
    all_decay = lax.all_gather(block_decay[None], "ctx", axis=0, tiled=True)
    ends_incl = jnp.cumsum(all_decay, axis=0)
    ends_excl = ends_incl - all_decay
    my_index = lax.axis_index("ctx")
    mine_incl = lax.dynamic_index_in_dim(ends_incl, my_index, 0, keepdims=False)
    mine_excl = lax.dynamic_index_in_dim(ends_excl, my_index, 0, keepdims=False)
    shard_part = lax.all_gather(summary[None], "ctx", axis=0, tiled=True)
    piece_rows = shard_part.shape[0]
    sources = jnp.arange(piece_rows)
    their_totals = ends_incl
    exponent = mine_excl[None] - their_totals
    weights = jnp.where(
        (sources < my_index)[:, None, None], jnp.exp(jnp.minimum(exponent, 0.0)), 0.0
    )
    prior = jnp.sum(shard_part * heads_wide(weights, head_size)[..., None], axis=0)
    decay_here = jnp.exp(heads_wide(cumulative, head_size))
    readout = jnp.einsum("stn,spn->stp", outflow_wide, prior, precision=HIGHEST)
    outer_part = readout * decay_here
    output_y = inner_part + outer_part + heads_wide(skip_gain, head_size) * signal
    gate_act = swish(gate_preactivation)
    gated = output_y * gate_act
    inverse_out = lax.rsqrt(jnp.mean(gated * gated, axis=-1, keepdims=True) + EPSILON)
    unit_out = gated * inverse_out
    normout = (unit_out * gate_gain).astype(jnp.bfloat16)
    projected = jnp.einsum("sle,em->slm", normout, out_weight, preferred_element_type=jnp.float32)
    result = (hidden + projected).astype(jnp.bfloat16)
    upstream = cotangent.astype(jnp.float32)
    grad_out_weight = jnp.einsum(
        "sle,slm->em", normout, cotangent, preferred_element_type=jnp.float32
    )
    grad_norm_out = jnp.einsum(
        "slm,em->sle", cotangent, out_weight, preferred_element_type=jnp.float32
    )
    grad_gate_gain = jnp.sum(grad_norm_out * unit_out, axis=(0, 1))
    grad_gated = rms_back(grad_norm_out * gate_gain, unit_out, inverse_out)
    grad_y = (grad_gated * gate_act).astype(jnp.bfloat16)
    gradient_gate_preactivation = (grad_gated * output_y * swish_grad(gate_preactivation)).astype(
        jnp.bfloat16
    )
    grad_y_wide = grad_y.astype(jnp.float32)
    grad_skip = jnp.sum(head_sums(grad_y_wide * signal, head_count), axis=(0, 1))
    grad_signal = heads_wide(skip_gain, head_size) * grad_y_wide
    weighted_grad = grad_y_wide * decay_here
    grad_outflow = jnp.einsum("stp,spn->stn", weighted_grad, prior, precision=HIGHEST)
    grad_prior = jnp.einsum("stp,stn->spn", weighted_grad, outflow_wide, precision=HIGHEST)
    grad_cumulative = head_sums(grad_y_wide * outer_part, head_count)
    grad_y_heads = grad_y.reshape(seqs_here, length, head_count, head_size)
    grad_mixing = jnp.einsum(
        "sthp,suhp->shtu", grad_y_heads, driven_heads, preferred_element_type=jnp.float32
    )
    grad_driven = jnp.einsum(
        "shtu,sthp->suhp", mixing, grad_y_heads, preferred_element_type=jnp.float32
    ).reshape(seqs_here, length, inner_width)
    through = grad_mixing * factor
    grad_scores = jnp.sum(through, axis=1).astype(jnp.bfloat16)
    spread = through * scores[:, None]
    grad_cumulative = (
        grad_cumulative
        + jnp.sum(spread, axis=3).transpose(0, 2, 1)
        - jnp.sum(spread, axis=2).transpose(0, 2, 1)
    )
    grad_outflow = grad_outflow + jnp.einsum(
        "stu,sun->stn", grad_scores, inflow, preferred_element_type=jnp.float32
    )
    grad_inflow = jnp.einsum(
        "stu,stn->sun", grad_scores, outflow, preferred_element_type=jnp.float32
    )
    shard_part = lax.all_gather(grad_prior[None], "ctx", axis=0, tiled=True)
    piece_rows = shard_part.shape[0]
    sources = jnp.arange(piece_rows)
    their_totals = ends_excl
    exponent = their_totals - mine_incl[None]
    weights = jnp.where(
        (sources > my_index)[:, None, None], jnp.exp(jnp.minimum(exponent, 0.0)), 0.0
    )
    later_grad = jnp.sum(shard_part * heads_wide(weights, head_size)[..., None], axis=0)
    grad_block_decay = jnp.exp(block_decay) * head_sums(
        jnp.sum(later_grad * prior, axis=-1), head_count
    )
    grad_scaled = jnp.einsum("spn,sun->sup", later_grad, inflow_wide, precision=HIGHEST)
    grad_inflow = grad_inflow + jnp.einsum(
        "sup,spn->sun", scaled.astype(jnp.float32), later_grad, precision=HIGHEST
    )
    grad_signal = grad_signal + grad_scaled * step_wide * tail_wide + grad_driven * step_wide
    grad_step = head_sums(grad_scaled * signal * tail_wide, head_count) + head_sums(
        grad_driven * signal, head_count
    )
    grad_tail = head_sums(grad_scaled * signal * step_wide, head_count) * tail
    grad_block_decay = grad_block_decay + jnp.sum(grad_tail, axis=1)
    grad_cumulative = grad_cumulative - grad_tail
    grad_cumulative = jnp.concatenate(
        [grad_cumulative[:, :-1], grad_cumulative[:, -1:] + grad_block_decay[:, None]], axis=1
    )
    grad_rate_terms = jnp.flip(jnp.cumsum(jnp.flip(grad_cumulative, 1), axis=1), 1)
    grad_step = grad_step + grad_rate_terms * rates
    grad_log_rates = rates * jnp.sum(grad_rate_terms * step_size, axis=(0, 1))
    grad_raw = grad_step * jax.nn.sigmoid(step_preactivation + step_bias)
    grad_step_bias = jnp.sum(grad_raw, axis=(0, 1))
    gradient_unprocessed_reduced = grad_raw.astype(jnp.bfloat16)
    grad_activated = jnp.concatenate([grad_signal, grad_inflow, grad_outflow], axis=-1)
    grad_filtered = grad_activated * swish_grad(filtered)
    grad_conv_bias = jnp.sum(grad_filtered, axis=(0, 1))
    grad_conv_weight = jnp.stack(
        [
            jnp.sum(grad_filtered * extended[:, offset : offset + length], axis=(0, 1))
            for offset in range(window + 1)
        ]
    )
    grad_extended = jnp.zeros(extended.shape, jnp.float32)
    for offset in range(window + 1):
        grad_extended = grad_extended + jnp.pad(
            conv_weight[offset] * grad_filtered, ((0, 0), (offset, window - offset), (0, 0))
        )
    returned = passed_along(grad_extended[:, :window].astype(jnp.bfloat16), "ctx", -1).astype(
        jnp.float32
    )
    grad_mixed = grad_extended[:, window:] + jnp.pad(
        returned, ((0, 0), (length - window, 0), (0, 0))
    )
    gradient_mixed_reduced = grad_mixed.astype(jnp.bfloat16)
    grad_normed = (
        jnp.einsum(
            "ptn,on->pto",
            gradient_gate_preactivation,
            gate_projection_matrix,
            preferred_element_type=jnp.float32,
        )
        + jnp.einsum(
            "ptn,on->pto",
            gradient_mixed_reduced,
            mixer_projection_matrix,
            preferred_element_type=jnp.float32,
        )
        + jnp.einsum(
            "ptn,on->pto",
            gradient_unprocessed_reduced,
            step_projection_matrix,
            preferred_element_type=jnp.float32,
        )
    )
    grad_gate_weight = jnp.einsum(
        "fgn,fgh->nh",
        normalized_input,
        gradient_gate_preactivation,
        preferred_element_type=jnp.float32,
    )
    grad_mixer_weight = jnp.einsum(
        "fgn,fgh->nh", normalized_input, gradient_mixed_reduced, preferred_element_type=jnp.float32
    )
    grad_step_weight = jnp.einsum(
        "fgn,fgh->nh",
        normalized_input,
        gradient_unprocessed_reduced,
        preferred_element_type=jnp.float32,
    )
    grad_norm_gain = jnp.sum(grad_normed * unit_in, axis=(0, 1))
    grad_hidden = rms_back(grad_normed * norm_gain, unit_in, inverse)
    token_grad = (upstream + grad_hidden).astype(jnp.bfloat16)
    summed = lax.psum(
        (
            grad_norm_gain,
            grad_gate_weight,
            grad_mixer_weight,
            grad_step_weight,
            grad_conv_weight,
            grad_conv_bias,
            grad_step_bias,
            grad_log_rates,
            grad_skip,
            grad_gate_gain,
            grad_out_weight,
        ),
        ("seq", "ctx"),
    )
    return (result, token_grad) + tuple(summed)


def solution(mesh):
    in_specs = (
        P("seq", "ctx", None),
        P(),
        P(),
        P(),
        P(),
        P(),
        P(),
        P(),
        P(),
        P(),
        P(),
        P(),
        P("seq", "ctx", None),
    )
    out_specs = (
        P("seq", "ctx", None),
        P("seq", "ctx", None),
        P(),
        P(),
        P(),
        P(),
        P(),
        P(),
        P(),
        P(),
        P(),
        P(),
        P(),
    )
    return jax.shard_map(
        on_device, mesh=mesh, in_specs=in_specs, out_specs=out_specs, check_vma=False
    )
```

profile of v0, /device:TPU:0, one launch (start us, length us, event | category | flops | bytes accessed | tf_op | source)
XLA Modules:
  0.0 723.9 jit_solution(6120748819458482183)
XLA Ops:
  61.8 12.6 %all-gather.1 = f32[16,1,24]{2,1,0:T(1,128)S(1)} all-gather(f32[2,1,24]{2,1,0:T(1,128)} %bitcast.168), channel_id=3, replica_groups=mesh['seq'=4,'ctx'=8] {'ctx'}, dimensions={0}, use_global_device_ids=true | all-gather | bytes 1728 | tf_op jit(solution)/shard_map/all_gather | solution.py:105
  82.1 4.0 copy.252
  90.5 6.2 fusion.2
  100.2 79.0 %all-gather.6.cloned.1.call-done = f32[16,1536,128]{2,1,0:T(8,128)} async-done(((f32[2,1536,128]{2,1,0:T(8,128)}), f32[16,1536,128]{2,1,0:T(8,128)}) %all-gather.6.cloned.1.call-update) | async-done | bytes 12582928 | tf_op jit(solution)/shard_map/all_gather | solution.py:111
  179.2 8.2 %multiply_reduce_fusion.1 = f32[2,1536,128]{2,1,0:T(8,128)S(1)} fusion(f32[8,2,1536,128]{3,2,1,0:T(8,128)} %bitcast.146, f32[8,2,1536]{2,1,0:T(2,128)} %mul.353), kind=kLoop, calls=%fused_computation.1 | loop fusion | flops 5898240 | bytes 14254080 | tf_op jit(solution)/shard_map/reduce_sum | solution.py:119
  194.0 5.2 multiply_reduce_fusion.8
  199.2 4.1 fusion.8
  204.5 4.8 fusion.26
  215.3 9.9 %multiply_reduce_fusion.3 = (f32[2,24,256]{2,1,0:T(8,128)}, f32[2,24,256]{2,1,0:T(8,128)}, bf16[2,256,256]{2,1,0:T(8,128)(2,1)}) fusion(f32[2,256,256]{2,1,0:T(8,128)} %copy-done.27, f32[2,24,256]{2,1,0:T(8,128)} %copy_bitcast_fusion, pred[256,256]{1,0:T(8,128)(4,1)} %iota_compare_fusion, bf16[2,256,24,64]{1,3,2,0:T(8,128)(2,1)} %bitcast.161, ...), kind=kOutput, calls=%fused_computation.6 | convolution fusion | flops 427663360 | bytes 4145152 | tf_op jit(solution)/shard_map/sthp,suhp->shtu/dot_general | solution.py:152
  228.5 6.2 fusion.1
  240.2 5.8 fusion.25
  247.9 3.7 convolution_bitcast_fusion.2
  251.6 3.7 convolution_bitcast_fusion
  255.4 69.1 %all-gather.8.cloned.1.call-done = f32[16,1536,128]{2,1,0:T(8,128)} async-done(((f32[2,1536,128]{2,1,0:T(8,128)}), f32[16,1536,128]{2,1,0:T(8,128)}) %all-gather.8.cloned.1.call-update) | async-done | bytes 12582928 | tf_op jit(solution)/shard_map/all_gather | solution.py:172
  324.4 8.0 %multiply_reduce_fusion = f32[2,1536,128]{2,1,0:T(8,128)S(1)} fusion(f32[8,2,1536,128]{3,2,1,0:T(8,128)} %bitcast.147, f32[8,2,1536]{2,1,0:T(2,128)} %mul.379), kind=kLoop, calls=%fused_computation | loop fusion | flops 5898240 | bytes 14254080 | tf_op jit(solution)/shard_map/reduce_sum | solution.py:180
  337.5 4.2 convolution_add_fusion.1
  341.6 13.9 %fusion.42 = (f32[2,256,1536]{2,1,0:T(8,128)}, f32[2,256,1536]{2,1,0:T(8,128)}, f32[2,256,1536]{2,1,0:T(8,128)}, f32[2,256,1536]{2,1,0:T(8,128)}, f32[2,256,1536]{2,1,0:T(8,128)}) fusion(f32[2,256,1536]{2,1,0:T(8,128)} %copy.248, f32[2,256,1792]{2,1,0:T(8,128)S(1)} %copy-done.5, f32[2,256,1536]{2,1,0:T(8,128)} %copy.242, f32[2,256,1536]{2,1,0:T(8,128)} %copy.259, ...), kind=kOutput, calls=%fused_computation.85 | convolution fusion | flops 1217396736 | bytes 34742272 | tf_op jit(solution)/shard_map/spn,sun->sup/dot_general | solution.py:184
  412.8 10.5 %multiply_reduce_fusion.7 = (f32[1792]{0:T(1024)}, f32[1792]{0:T(1024)}, f32[1792]{0:T(1024)}, f32[1792]{0:T(1024)}, f32[1792]{0:T(1024)}, /*index=5*/f32[2,256,1792]{2,1,0:T(8,128)S(1)}) fusion(f32[2,259,1792]{2,1,0:T(8,128)} %copy-done.1, f32[2,256,1792]{2,1,0:T(8,128)} %get-tuple-element.54, f32[2,256,128]{2,1,0:T(8,128)} %convolution_add_fusion, ...), kind=kLoop, calls=%fused_computation.24 | loop fusion | flops 17423616 | bytes 25725952 | tf_op jit(solution)/shard_map/reduce_sum | solution.py:209
  426.4 5.3 pad_add_fusion
  436.9 6.2 convolution_bitcast_fusion.1
  454.6 3.7 fusion.33
  458.3 44.2 %all-reduce.5 = (f32[768]{0:T(1024)}, f32[4,1792]{1,0:T(4,128)}, f32[1792]{0:T(1024)}, f32[24]{0:T(128)}, f32[24]{0:T(128)}, /*index=5*/f32[24]{0:T(128)}, f32[1536]{0:T(1024)}) all-reduce(f32[768]{0:T(1024)} %get-tuple-element.23, f32[4,1792]{1,0:T(4,128)} %pad_maximum_fusion.1, ...), channel_id=1, replica_groups=mesh['seq'=4,'ctx'=8] {'seq','ctx'}, use_global_device_ids=true, to_apply=%region_22.23 | all-reduce | flops 11336 | bytes 90688 | tf_op jit(solution)/shard_map/psum | solution.py:263
  506.3 199.2 %all-reduce.9.cloned.1.call-done = (f32[768,1536]{1,0:T(8,128)}, f32[768,1792]{1,0:T(8,128)}, f32[768,24]{0,1:T(8,128)}, f32[1536,768]{1,0:T(8,128)}) async-done(((f32[768,1536]{1,0:T(8,128)}, f32[768,1792]{1,0:T(8,128)}, f32[768,24]{0,1:T(8,128)}, f32[1536,768]{1,0:T(8,128)}), (f32[768,1536]{1,0:T(8,128)}, f32[768,1792]{1,0:T(8,128)}, f32[768,24]{0,1:T(8,128)}, ...) | async-done | bytes 15015952 | tf_op jit(solution)/shard_map/psum | solution.py:263
  705.5 5.2 copy.315
  (266 shorter events, 186.0 us)
Async XLA Ops:
  7.2 172.0 %all-gather.6.cloned.1.call-start = ((), (), s32[]{:S(2)}) async-start(), calls=%async_computation | async-start | bytes 14155776 | tf_op jit(solution)/shard_map/all_gather | solution.py:111
  9.2 7.8 %copy-start.50 = (f32[2,256]{1,0:T(2,128)}, f32[2,256]{1,0:T(2,128)S(1)}, u32[]{:S(2)}) copy-start(f32[2,256]{1,0:T(2,128)S(1)} %add_rsqrt_fusion.1) | copy-start | bytes 6148
  9.2 7.7 %copy-start.71 = (f32[24]{0:T(128)S(1)}, f32[24]{0:T(128)}, u32[]{:S(2)}) copy-start(f32[24]{0:T(128)} %param.21) | copy-start | bytes 292
  9.2 7.8 %copy-start.17 = (bf16[2,256,768]{2,1,0:T(8,128)(2,1)S(1)}, bf16[2,256,768]{2,1,0:T(8,128)(2,1)}, u32[]{:S(2)}) copy-start(bf16[2,256,768]{2,1,0:T(8,128)(2,1)} %param.13) | copy-start | bytes 2359300
  9.2 7.8 %copy-start.34 = (f32[768]{0:T(1024)S(1)}, f32[768]{0:T(1024)}, u32[]{:S(2)}) copy-start(f32[768]{0:T(1024)} %param.14) | copy-start | bytes 9220
  9.2 7.8 %copy-start.48 = (bf16[768,24]{0,1:T(8,128)(2,1)S(1)}, bf16[768,24]{0,1:T(8,128)(2,1)}, u32[]{:S(2)}) copy-start(bf16[768,24]{0,1:T(8,128)(2,1)} %param.17) | copy-start | bytes 110596
  9.2 7.8 %copy-start.70 = (f32[24]{0:T(128)S(1)}, f32[24]{0:T(128)}, u32[]{:S(2)}) copy-start(f32[24]{0:T(128)} %param.20) | copy-start | bytes 292
  14.0 31.8 %collective-permute-start = (bf16[2,3,1792]{2,1,0:T(4,128)(2,1)}, bf16[2,3,1792]{2,1,0:T(4,128)(2,1)}, u32[]{:S(2)}, u32[]{:S(2)}) collective-permute-start(bf16[2,3,1792]{2,1,0:T(4,128)(2,1)} %slice.95), channel_id=1, source_target_pairs={{0,1},{1,2},{2,3},{3,4},{4,5},{5,6},{6,7},{8,9},{9,10},{10,11},{11... | collective-permute-start | bytes 64520 | tf_op jit(solution)/shard_map/ppermute | solution.py:13
  31.5 16.2 %copy-start.38 = (f32[1792]{0:T(1024)}, f32[1792]{0:T(1024)S(1)}, u32[]{:S(2)}) copy-start(f32[1792]{0:T(1024)S(1)} %get-tuple-element.25) | copy-start | bytes 21508
  60.3 264.1 %all-gather.8.cloned.1.call-start = ((), (), s32[]{:S(2)}) async-start(), calls=%async_computation.1 | async-start | bytes 14155776 | tf_op jit(solution)/shard_map/all_gather | solution.py:172
  179.2 9.4 %copy-start.2 = (f32[2,256,1536]{2,1,0:T(8,128)S(1)}, f32[2,256,1536]{2,1,0:T(8,128)}, u32[]{:S(2)}) copy-start(f32[2,256,1536]{2,1,0:T(8,128)} %copy.252) | copy-start | bytes 9437188
  179.2 12.0 %copy-start.66 = (bf16[768,1536]{1,0:T(8,128)(2,1)S(1)}, bf16[768,1536]{1,0:T(8,128)(2,1)}, u32[]{:S(2)}) copy-start(bf16[768,1536]{1,0:T(8,128)(2,1)} %param.15) | copy-start | bytes 7077892
  209.3 496.2 %all-reduce.9.cloned.1.call-start = ((), (), s32[]{:S(2)}) async-start(), calls=%async_computation.2 | async-start | bytes 30031872 | tf_op jit(solution)/shard_map/psum | solution.py:263
  240.2 7.7 %copy-start.18 = (bf16[2,256,1536]{2,1,0:T(8,128)(2,1)S(1)}, bf16[2,256,1536]{2,1,0:T(8,128)(2,1)}, u32[]{:S(2)}) copy-start(bf16[2,256,1536]{2,1,0:T(8,128)(2,1)} %get-tuple-element.55) | copy-start | bytes 4718596
  324.4 9.2 %copy-start.10 = (f32[2,1536,128]{2,1,0:T(8,128)S(1)}, f32[2,1536,128]{2,1,0:T(8,128)}, u32[]{:S(2)}) copy-start(f32[2,1536,128]{2,1,0:T(8,128)} %copy-done.9) | copy-start | bytes 4718596
  412.8 10.5 %copy-start.39 = (f32[1792]{0:T(1024)S(1)}, f32[1792]{0:T(1024)}, u32[]{:S(2)}) copy-start(f32[1792]{0:T(1024)} %copy-done.38) | copy-start | bytes 21508
  412.8 10.5 %copy-start.41 = (f32[1792]{0:T(1024)S(1)}, f32[1792]{0:T(1024)}, u32[]{:S(2)}) copy-start(f32[1792]{0:T(1024)} %get-tuple-element.26) | copy-start | bytes 21508
  412.8 10.5 %copy-start.43 = (f32[1792]{0:T(1024)S(1)}, f32[1792]{0:T(1024)}, u32[]{:S(2)}) copy-start(f32[1792]{0:T(1024)} %get-tuple-element.27) | copy-start | bytes 21508
  412.8 10.5 %copy-start.45 = (f32[1792]{0:T(1024)S(1)}, f32[1792]{0:T(1024)}, u32[]{:S(2)}) copy-start(f32[1792]{0:T(1024)} %get-tuple-element.28) | copy-start | bytes 21508
  426.3 7.6 %copy-start.33 = (f32[2,256,24]{1,2,0:T(8,128)S(1)}, f32[2,256,24]{1,2,0:T(8,128)}, u32[]{:S(2)}) copy-start(f32[2,256,24]{1,2,0:T(8,128)} %reduce_sum.256) | copy-start | bytes 147460
  426.4 7.6 %copy-start.61 = (u8[256,24]{0,1:T(8,128)(4,1)S(1)}, u8[256,24]{0,1:T(8,128)(4,1)}, u32[]{:S(2)}) copy-start(u8[256,24]{0,1:T(8,128)(4,1)} %copy-done.60) | copy-start | bytes 18436
  426.4 7.6 %copy-start.64 = (f32[24]{0:T(128)S(1)}, f32[24]{0:T(128)}, u32[]{:S(2)}) copy-start(f32[24]{0:T(128)} %copy-done.63) | copy-start | bytes 292
  432.6 3.7 collective-permute-start.1
  705.5 9.3 %slice-start = ((s8[4718592]{0:T(1024)(128)(4,1)}), s8[4194304]{0:T(1024)(128)(4,1)S(1)}, s32[]{:S(2)}) async-start(s8[4718592]{0:T(1024)(128)(4,1)} %bitcast.155), calls=%async_computation.3 | async-start | bytes 8388608
  (56 other events, 186.1 us)
Sparse Core Ops, SparseCore 0:
  60.4 118.7 all-gather.5
  209.4 114.9 all-gather.7
  443.3 262.1 all-reduce.8
where the time goes:
time: 733 us; the launch traced here: 724 us
  waiting for transfers between devices  347 us (47%)
  local copies, waits for them, and re-layouts  111 us (15%)
  matrix products  96.1 us (13%)
  other arithmetic  93.1 us (13%)
  blocking collectives  56.8 us (8%)
  between operations  14.9 us (2%)
    psum x1, waiting for transfers between devices, on_device(): lax.psum((grad_norm_gain, grad_gate_weight, grad_mixer_weight, grad_step_...  199 us
    all_gather x1, waiting for transfers between devices, on_device(): shard_part = lax.all_gather(summary[None], 'ctx', axis=0, tiled=True)  79 us
    all_gather x1, waiting for transfers between devices, on_device(): shard_part = lax.all_gather(grad_prior[None], 'ctx', axis=0, tiled=True)  69.1 us
    psum x1, blocking collectives, on_device(): lax.psum((grad_norm_gain, grad_gate_weight, grad_mixer_weight, grad_step_...  44.2 us
    unnamed x155, local copies, waits for them, and re-layouts  26.6 us
    reduce_sum x2, other arithmetic, on_device(): jnp.sum(shard_part * heads_wide(weights, head_size)[..., None], axis=0)  16.2 us
  transfers between devices with their start and end apart: 5, of which 3 were waited for; matrix products, arithmetic and copies ran while one was open for 17% of the time, Pallas kernels for 0%

commit v1 on v0

v1 whole, which is shorter than its diff:
```python
import functools

import jax
import jax.numpy as jnp
from jax import lax
from jax.experimental import pallas as pl
from jax.experimental.pallas import tpu as pltpu
from jax.sharding import PartitionSpec as P

MESH = pl.DeviceIdType.MESH
BF = jnp.bfloat16
F32 = jnp.float32
EPSILON = 1e-05
BW = 256
LN = 128


def dot(a, b):
    return jnp.dot(a, b, preferred_element_type=F32)


def dot_nt(a, b):
    return lax.dot_general(a, b, (((1,), (1,)), ((), ())), preferred_element_type=F32)


def split2(v):
    hi = v.astype(BF)
    return hi, (v - hi.astype(F32)).astype(BF)


def split3(v):
    hi = v.astype(BF)
    rest = v - hi.astype(F32)
    mid = rest.astype(BF)
    return hi, mid, (rest - mid.astype(F32)).astype(BF)


def dot3(a, v):
    hi, mid, lo = split3(v)
    return dot(a, hi) + dot(a, mid) + dot(a, lo)


def pieces3(v):
    lane = lax.broadcasted_iota(jnp.int32, v.shape, 1)
    hi, mid, lo = split3(v)
    z = jnp.zeros_like(v)
    return jnp.where(
        lane < 32,
        hi.astype(F32),
        jnp.where(lane < 64, mid.astype(F32), jnp.where(lane < 96, lo.astype(F32), z)),
    ).astype(BF)


def sigmoid(v):
    return 1.0 / (1.0 + jnp.exp(-v))


def ds(start, size):
    return pl.ds(pl.multiple_of(start, size), size)


def layer_kernel(
    nctx,
    tok_h, ng_r, wg_h, wm_h, ws_r, cw_r, cb_r, sb_r, lr_r, sk_r, gg_r, wo_h, cot_h,
    res_r, tg_r, go_h, gw_h, gm_h, small_r, stepg_r,
    tok, cot, wg, wm, wo, halo, ne, nt, ext, fil, drv, scl, y, z, big, gy, ggz, nrm, nrt,
    acc_a, acc_b, gn, sum_s, out_f, in_f, out_b, in_b, sraw, st, cum, cum_t, pst, ptl, pdc,
    dlast, infl, outf, inf_t, outf_t, sco, sco_t, gsc, xx, tri, ginf, gout, hs_d, hs_g, bdh,
    skw, gstage,
    in_sem, out_sem, st_sem, halo_s, halo_r, fs_s, fs_r, bs_s, bs_r, gh_s, gh_r,
):
    seqs, length, dm = tok.shape
    di = wg.shape[1]
    xbc = wm.shape[1]
    heads = ws_r.shape[1]
    hp = di // heads
    nst = (xbc - di) // 2
    window = cw_r.shape[0] - 1
    nblk = di // BW
    nchunk = di // LN
    hw = 16
    seq = lax.axis_index("seq")
    ctx = lax.axis_index("ctx")
    has_prev = ctx > 0
    has_next = ctx < nctx - 1
    prv = (seq, ctx - 1)
    nxt = (seq, ctx + 1)

    barrier = pltpu.get_barrier_semaphore()

    @pl.when(has_prev)
    def _():
        pl.semaphore_signal(barrier, inc=1, device_id=prv, device_id_type=MESH)

    @pl.when(has_next)
    def _():
        pl.semaphore_signal(barrier, inc=1, device_id=nxt, device_id_type=MESH)

    loads = [
        pltpu.make_async_copy(a, b, in_sem.at[i])
        for i, (a, b) in enumerate(
            ((tok_h, tok), (wm_h, wm), (cot_h, cot), (wo_h, wo), (wg_h, wg))
        )
    ]
    for copy in loads:
        copy.start()

    pl.semaphore_wait(barrier, has_prev.astype(jnp.int32) + has_next.astype(jnp.int32))
    loads[0].wait()

    halo_copy = pltpu.make_async_remote_copy(
        src_ref=tok.at[:, pl.ds(length - hw, hw), :], dst_ref=halo, send_sem=halo_s,
        recv_sem=halo_r, device_id=nxt, device_id_type=MESH,
    )

    @pl.when(has_next)
    def _():
        halo_copy.start()

    @pl.when(jnp.logical_not(has_prev))
    def _():
        halo[...] = jnp.zeros_like(halo)
        in_f[...] = jnp.zeros_like(in_f)

    @pl.when(jnp.logical_not(has_next))
    def _():
        in_b[...] = jnp.zeros_like(in_b)

    lane128 = lax.broadcasted_iota(jnp.int32, (1, LN), 1)
    r_i = lax.broadcasted_iota(jnp.int32, (LN, di), 0)
    c_i = lax.broadcasted_iota(jnp.int32, (LN, di), 1)
    xx[...] = jnp.where((r_i % 32 == c_i // hp) & (r_i < 96), 1.0, 0.0).astype(BF)
    t_r = lax.broadcasted_iota(jnp.int32, (length, length), 0)
    t_c = lax.broadcasted_iota(jnp.int32, (length, length), 1)
    tri[0] = jnp.where(t_r >= t_c, 1.0, 0.0).astype(BF)
    tri[1] = jnp.where(t_r <= t_c, 1.0, 0.0).astype(BF)
    k_i = lax.broadcasted_iota(jnp.int32, (heads, LN), 0)
    l_i = lax.broadcasted_iota(jnp.int32, (heads, LN), 1)
    rep = jnp.where((l_i % 32 == k_i) & (l_i < 96), 1.0, 0.0)

    def replicated(row_ref):
        row = jnp.broadcast_to(row_ref[...].reshape(1, heads), (8, heads))
        hi, mid, lo = split3(row)
        r = rep.astype(BF)
        return (dot(hi, r) + dot(mid, r) + dot(lo, r))[0:1]

    ws3 = dot(ws_r[...], rep.astype(BF)).astype(BF)
    bias3 = replicated(sb_r)
    rates3 = -jnp.exp(replicated(lr_r))
    sk8 = jnp.broadcast_to(replicated(sk_r), (8, LN))
    skw[...] = dot(pieces3(sk8), xx[...])

    gain = ng_r[...].reshape(1, dm)

    def norm_rows(rows):
        v = rows.astype(F32)
        inv = lax.rsqrt(jnp.mean(v * v, axis=-1, keepdims=True) + EPSILON)
        return ((v * inv) * gain).astype(BF)

    for s in range(seqs):

        def norm_body(i, _, s=s):
            ne[s, ds(hw + i * 16, 16), :] = norm_rows(tok[s, ds(i * 16, 16), :])
            return 0

        lax.fori_loop(0, length // 16, norm_body, 0, unroll=2)

    for s in range(seqs):
        raw = dot(ne[s, pl.ds(hw, length), :], ws3)
        sraw[s] = raw
        step = jax.nn.softplus(raw + bias3)
        st[s] = step
        cu = dot3(tri[0], step * rates3)
        cum[s] = cu
        cum_t[s] = cu.T
        last = cu[length - 1 : length]
        pst[s] = pieces3(step)
        ptl[s] = pieces3(jnp.exp(last - cu))
        dec = jnp.exp(cu)
        pdc[s] = pieces3(dec)
        dlast[s] = dot(pieces3(dec[length - 8 :]), xx[...])

    for s in range(seqs):
        for b in range(dm // BW):
            nt[b * BW : (b + 1) * BW, s * length : (s + 1) * length] = ne[
                s, hw : hw + length, b * BW : (b + 1) * BW
            ].T

    @pl.when(has_prev)
    def _():
        halo_copy.wait_recv()

    for s in range(seqs):
        ne[s, 0:hw, :] = norm_rows(halo[s])

    loads[1].wait()

    def filter_block(b, s):
        cols = ds(b * BW, BW)
        m = dot(ne[s], wm[:, cols]).astype(BF)
        ext[s, :, cols] = m
        m = m.astype(F32)
        f = cb_r[cols].reshape(1, BW)
        for k in range(window + 1):
            shift = window - k
            moved = pltpu.roll(m, shift, 0) if shift else m
            f = f + cw_r[k : k + 1, cols] * moved[hw:]
        fil[s, :, cols] = f
        return f

    for s in range(seqs):
        f = filter_block(nblk, s)
        act = f * sigmoid(f)
        i_bf = act[:, :nst].astype(BF)
        o_bf = act[:, nst:].astype(BF)
        infl[s] = i_bf
        outf[s] = o_bf
        inf_t[s] = i_bf.T
        outf_t[s] = o_bf.T
        sco[s] = dot_nt(o_bf, i_bf)
        sco_t[s] = dot_nt(i_bf, o_bf)

    def signal_body(b, _):
        cols = ds(b * BW, BW)
        for s in range(seqs):
            f = filter_block(b, s)
            sig = f * sigmoid(f)
            x = xx[:, cols]
            dr = sig * dot(pst[s], x)
            drv[s, :, cols] = dr.astype(BF)
            sc = (dr * dot(ptl[s], x)).astype(BF)
            scl[s, :, cols] = sc
            y[s, :, cols] = skw[0:1, cols] * sig
            summ = dot(inf_t[s], sc)
            sum_s[2 * b, s] = summ[:, :LN]
            sum_s[2 * b + 1, s] = summ[:, LN:]
        return 0

    lax.fori_loop(0, nblk, signal_body, 0)

    def relay(c, in_buf, out_buf, sems, has_in, has_out, to):
        copy = pltpu.make_async_remote_copy(
            src_ref=out_buf.at[c], dst_ref=in_buf.at[c], send_sem=sems[0].at[c],
            recv_sem=sems[1].at[c], device_id=to, device_id_type=MESH,
        )

        @pl.when(has_in)
        def _():
            copy.wait_recv()

        @pl.when(has_out)
        def _():
            for s in range(seqs):
                row = dlast[s, 7:8, ds(c * LN, LN)]
                out_buf[c, s] = (row * in_buf[c, s].astype(F32) + sum_s[c, s]).astype(out_buf.dtype)
            copy.start()

    def relay_slot(slot, skew, *rest):
        c = slot - skew

        @pl.when((c >= 0) & (c < nchunk))
        def _():
            relay(c, *rest)

    half = length // 2
    d_r = lax.broadcasted_iota(jnp.int32, (half, half), 0)
    d_c = lax.broadcasted_iota(jnp.int32, (half, half), 1)
    NEG = -1e30

    def columns_of(s, j):
        moved = pltpu.roll(cum[s], lax.rem(LN - 2 * j, LN), 1)
        return moved[:, 0:1], moved[:, 1:2]

    def pair_forward(j, s):
        cols = ds(j * LN, LN)
        d = drv[s, :, cols]
        lane_low = lane128 < hp
        top, bottom = [], []
        for hh, col in enumerate(columns_of(s, j)):
            row = cum_t[s, pl.ds(2 * j + hh, 1), :]
            fa = jnp.exp(jnp.where(d_r >= d_c, col[:half] - row[:, :half], NEG))
            fb = jnp.exp(col[half:] - row[:, :half])
            fc = jnp.exp(jnp.where(d_r >= d_c, col[half:] - row[:, half:], NEG))
            top.append((sco[s, :half, :half] * fa).astype(BF))
            bottom.append(
                jnp.concatenate(
                    [
                        (sco[s, half:, :half] * fb).astype(BF),
                        (sco[s, half:, half:] * fc).astype(BF),
                    ],
                    axis=1,
                )
            )
        lo = dot(jnp.concatenate(top, axis=0), d[:half])
        hi = dot(jnp.concatenate(bottom, axis=0), d)
        y[s, :half, cols] += jnp.where(lane_low, lo[:half], lo[half:])
        y[s, half:, cols] += jnp.where(lane_low, hi[:half], hi[half:])

    loads[2].wait()
    loads[3].wait()
    loads[4].wait()

    fskew = (3 * ctx) // 2
    bskew = (3 * (nctx - 1 - ctx)) // 2
    slots = nchunk + (3 * (nctx - 1)) // 2

    f_args = (in_f, out_f, (fs_s, fs_r), has_prev, has_next, nxt)
    b_args = (in_b, out_b, (bs_s, bs_r), has_next, has_prev, prv)

    def forward_body(b, _):
        cols = ds(b * BW, BW)
        relay_slot(2 * b, fskew, *f_args)
        for s in range(seqs):
            big[s, 0:length, cols] = dot_nt(cot[s], wo[cols, :])
            pair_forward(2 * b, s)
        relay_slot(2 * b + 1, fskew, *f_args)
        for s in range(seqs):
            z[s, :, cols] = dot(ne[s, hw : hw + length, :], wg[:, cols])
            pair_forward(2 * b + 1, s)
        return 0

    lax.fori_loop(0, nblk, forward_body, 0)

    def forward_rest(slot, _):
        relay_slot(slot, fskew, *f_args)
        return 0

    lax.fori_loop(nchunk, slots, forward_rest, 0)

    acc_a[...] = jnp.zeros_like(acc_a)
    acc_b[...] = jnp.zeros_like(acc_b)

    def gate_body(b, _):
        cols = ds(b * BW, BW)
        for s in range(seqs):
            pr = jnp.concatenate([in_f[2 * b, s], in_f[2 * b + 1, s]], axis=1)
            phi, plo = split2(pr)
            out = (dot(outf[s], phi) + dot(outf[s], plo)) * dot(pdc[s], xx[:, cols])
            yy = y[s, :, cols] + out
            y[s, :, cols] = yy
            zz = z[s, :, cols]
            gated = yy * (zz * sigmoid(zz))
            q = big[s, 0:length, cols] * gg_r[cols].reshape(1, BW)
            a = gated * gated
            c = q * gated
            acc_a[s] += a[:, :LN] + a[:, LN:]
            acc_b[s] += c[:, :LN] + c[:, LN:]
        return 0

    lax.fori_loop(0, nblk, gate_body, 0)

    inv_out, mean_out = [], []
    for s in range(seqs):
        iv = lax.rsqrt(jnp.sum(acc_a[s], axis=-1, keepdims=True) / di + EPSILON)
        inv_out.append(iv)
        mean_out.append(iv * jnp.sum(acc_b[s], axis=-1, keepdims=True) / di)
    gout[...] = jnp.zeros_like(gout)

    def grad_body(b, _):
        cols = ds(b * BW, BW)
        gg_sum = jnp.zeros((1, BW), F32)
        for s in range(seqs):
            yy = y[s, :, cols]
            zz = z[s, :, cols]
            sg = sigmoid(zz)
            act = zz * sg
            unit = (yy * act) * inv_out[s]
            gain_row = gg_r[cols].reshape(1, BW)
            g = big[s, 0:length, cols]
            no = (unit * gain_row).astype(BF)
            nrm[s, :, cols] = no
            nrt[cols, s * length : (s + 1) * length] = no.T
            gg_sum = gg_sum + jnp.sum(g * unit, axis=0, keepdims=True)
            gr = inv_out[s] * (g * gain_row - unit * mean_out[s])
            gyb = (gr * act).astype(BF)
            gy[s, :, cols] = gyb
            ggz[s, :, cols] = (gr * yy * (sg * (1.0 + zz * (1.0 - sg)))).astype(BF)
            w = gyb.astype(F32) * dot(pdc[s], xx[:, cols])
            whi, wlo = split2(w)
            pr = jnp.concatenate([in_f[2 * b, s], in_f[2 * b + 1, s]], axis=1)
            gp = dot(outf_t[s], whi) + dot(outf_t[s], wlo)
            sum_s[2 * b, s] = gp[:, :LN]
            sum_s[2 * b + 1, s] = gp[:, LN:]
            phi, plo = split2(pr)
            gout[s] += dot_nt(whi, phi) + (dot_nt(wlo, phi) + dot_nt(whi, plo))
        small_r[0:1, cols] = gg_sum
        return 0

    lax.fori_loop(0, nblk, grad_body, 0)

    gsc[...] = jnp.zeros_like(gsc)

    def pair_backward(j, s):
        cols = ds(j * LN, LN)
        d = drv[s, :, cols]
        g = gy[s, :, cols]
        lane_low = lane128 < hp
        zero = jnp.zeros_like(d)
        top, bottom = [], []
        t1 = t2 = t3 = None
        for hh, col in enumerate(columns_of(s, j)):
            row = cum_t[s, pl.ds(2 * j + hh, 1), :]
            dh = jnp.where(lane_low if hh == 0 else jnp.logical_not(lane_low), d, zero)
            m1 = dot_nt(dh[:half], g)
            m2 = dot_nt(dh[half:], g[half:])
            fa = jnp.exp(jnp.where(d_r <= d_c, row[:, :half] - col[:half], NEG))
            fb = jnp.exp(row[:, half:] - col[:half])
            fc = jnp.exp(jnp.where(d_r <= d_c, row[:, half:] - col[half:], NEG))
            top.append(
                jnp.concatenate(
                    [
                        (sco_t[s, :half, :half] * fa).astype(BF),
                        (sco_t[s, :half, half:] * fb).astype(BF),
                    ],
                    axis=1,
                )
            )
            bottom.append((sco_t[s, half:, half:] * fc).astype(BF))
            p1, p2, p3 = m1[:, :half] * fa, m1[:, half:] * fb, m2 * fc
            t1, t2, t3 = (p1, p2, p3) if hh == 0 else (t1 + p1, t2 + p2, t3 + p3)
        gsc[s, :half, :half] += t1
        gsc[s, :half, half:] += t2
        gsc[s, half:, half:] += t3
        lo = dot(jnp.concatenate(top, axis=0), g)
        hi = dot(jnp.concatenate(bottom, axis=0), g[half:])
        z[s, :half, cols] = jnp.where(lane_low, lo[:half], lo[half:])
        z[s, half:, cols] = jnp.where(lane_low, hi[:half], hi[half:])

    def stage_out(slot, value, dst):
        gstage[slot] = value
        copy = pltpu.make_async_copy(gstage.at[slot], dst, st_sem.at[slot])
        copy.start()
        copy.wait()

    def backward_body(b, _):
        cols = ds(b * BW, BW)
        relay_slot(2 * b, bskew, *b_args)
        both = jnp.concatenate([ggz[s, :, cols] for s in range(seqs)], axis=0)
        stage_out(0, dot(nt[...], both), gw_h.at[:, cols])
        rows = jnp.concatenate([cot[s] for s in range(seqs)], axis=0)
        t = dot(nrt[cols, :], rows)
        for i in range(dm // BW):
            gstage[1, i * BW : (i + 1) * BW] = t[:, i * BW : (i + 1) * BW]
        for i in range(dm // BW):
            copy = pltpu.make_async_copy(
                gstage.at[1, pl.ds(i * BW, BW)], go_h.at[cols, pl.ds(i * BW, BW)],
                st_sem.at[1],
            )
            copy.start()
            copy.wait()
        for s in range(seqs):
            pair_backward(2 * b, s)
        relay_slot(2 * b + 1, bskew, *b_args)
        for s in range(seqs):
            pair_backward(2 * b + 1, s)
        return 0

    lax.fori_loop(0, nblk, backward_body, 0)

    for s in range(seqs):
        for i in range(dm // BW):
            cols = slice(i * BW, (i + 1) * BW)
            pj = dot(nrm[s], wo[:, cols])
            res_r[s, :, cols] = (tok[s, :, cols].astype(F32) + pj).astype(BF)
            gn[s, :, cols] = dot_nt(ggz[s], wg[cols, :])

    def backward_rest(slot, _):
        relay_slot(slot, bskew, *b_args)
        return 0

    lax.fori_loop(nchunk, slots, backward_rest, 0)

    ginf[...] = jnp.zeros_like(ginf)
    hs_d[...] = jnp.zeros_like(hs_d)
    hs_g[...] = jnp.zeros_like(hs_g)
    bdh[...] = jnp.zeros_like(bdh)

    def head_sum(v, x):
        hi, lo = split2(v)
        return dot_nt(hi, x) + dot_nt(lo, x)

    def head_sum3(v, x):
        hi, mid, lo = split3(v)
        return dot_nt(hi, x) + dot_nt(mid, x) + dot_nt(lo, x)

    def gh_copy(b):
        cols = ds(b * BW, BW)
        return pltpu.make_async_remote_copy(
            src_ref=big.at[:, pl.ds(0, 8), cols], dst_ref=big.at[:, pl.ds(length, 8), cols],
            send_sem=gh_s.at[b], recv_sem=gh_r.at[b], device_id=prv, device_id_type=MESH,
        )

    @pl.when(jnp.logical_not(has_next))
    def _():
        big[:, length : length + 8, :] = jnp.zeros((seqs, 8, xbc), F32)

    def finish_block(b, s, ga):
        cols = ds(b * BW, BW)
        f = fil[s, :, cols]
        sg = sigmoid(f)
        gf = ga * (sg * (1.0 + f * (1.0 - sg)))
        big[s, 0:length, cols] = gf
        return jnp.sum(gf, axis=0, keepdims=True)

    def last_body(b, _):
        cols = ds(b * BW, BW)
        cb_sum = jnp.zeros((1, BW), F32)
        sk_sum = jnp.zeros((1, BW), F32)
        x = xx[:, cols]
        for s in range(seqs):
            lt = jnp.concatenate([in_b[2 * b, s], in_b[2 * b + 1, s]], axis=1)
            pr = jnp.concatenate([in_f[2 * b, s], in_f[2 * b + 1, s]], axis=1)
            f = fil[s, :, cols]
            sg = sigmoid(f)
            sig = f * sg
            stw = dot(pst[s], x)
            gst = dot(infl[s], lt) * dot(ptl[s], x)
            gd = z[s, :, cols]
            gyf = gy[s, :, cols].astype(F32)
            sk_row = skw[0:1, cols]
            gg = gst + gd
            ga = sk_row * gyf + stw * gg
            t1 = stw * sig * gst
            dd = gyf * (y[s, :, cols] - sk_row * sig) - drv[s, :, cols].astype(F32) * gd - t1
            hs_d[s] += head_sum(dd, x)
            hs_g[s] += head_sum(sig * gg, x)
            bd = jnp.sum(t1, axis=0, keepdims=True) + dlast[s, 7:8, cols] * jnp.sum(
                lt.astype(F32) * pr, axis=0, keepdims=True
            )
            bdh[s] += head_sum3(jnp.broadcast_to(bd, (8, BW)), x)
            sk_sum = sk_sum + jnp.sum(gyf * sig, axis=0, keepdims=True)
            ginf[s] += dot_nt(scl[s, :, cols], lt)
            gf = ga * (sg * (1.0 + f * (1.0 - sg)))
            big[s, 0:length, cols] = gf
            cb_sum = cb_sum + jnp.sum(gf, axis=0, keepdims=True)
        small_r[1:2, cols] = cb_sum
        small_r[2:3, cols] = sk_sum

        @pl.when(has_prev)
        def _():
            gh_copy(b).start()

        return 0

    lax.fori_loop(0, nblk, last_body, 0)

    cb_sum = jnp.zeros((1, BW), F32)
    for s in range(seqs):
        gst_bf = gsc[s].astype(BF)
        gi = ginf[s] + dot(gst_bf, outf[s])
        go = gout[s] + dot(gst_bf.T, infl[s])
        cb_sum = cb_sum + finish_block(nblk, s, jnp.concatenate([gi, go], axis=1))
    small_r[1:2, di:] = cb_sum

    @pl.when(has_prev)
    def _():
        gh_copy(nblk).start()

    row_i = lax.broadcasted_iota(jnp.int32, (length, LN), 0)
    glr = jnp.zeros((1, LN), F32)
    gsb = jnp.zeros((1, LN), F32)
    grl = []
    for s in range(seqs):
        gc = hs_d[s] + jnp.where(row_i == length - 1, bdh[s, 0:1], 0.0)
        terms = dot3(tri[1], gc)
        gst = hs_g[s] + terms * rates3
        glr = glr + jnp.sum(terms * st[s], axis=0, keepdims=True)
        graw = gst * sigmoid(sraw[s] + bias3)
        gsb = gsb + jnp.sum(graw, axis=0, keepdims=True)
        grl.append(jnp.where(lane128 < heads, graw, 0.0).astype(BF))
    small_r[3:4, 0:LN] = gsb
    small_r[4:5, 0:LN] = rates3 * glr
    sk_h = head_sum3(jnp.broadcast_to(small_r[2:3, :di], (8, di)), xx[...])
    small_r[5:6, 0:LN] = sk_h[0:1]
    stepg_r[...] = dot(nt[...], jnp.concatenate(grl, axis=0))

    def mixed_body(b, _):
        cols = ds(b * BW, BW)

        @pl.when(has_next)
        def _():
            gh_copy(b).wait_recv()

        parts = []
        sums = [jnp.zeros((1, BW), F32) for _ in range(window + 1)]
        for s in range(seqs):
            gf = big[s, :, cols]
            rows = gf.shape[0]
            m = ext[s, :, cols].astype(F32)
            gm = jnp.zeros((length, BW), F32)
            for k in range(window + 1):
                shift = window - k
                moved = pltpu.roll(gf, rows - shift, 0) if shift else gf
                gm = gm + cw_r[k : k + 1, cols] * moved[:length]
                em = pltpu.roll(m, shift, 0) if shift else m
                sums[k] = sums[k] + jnp.sum(gf[:length] * em[hw:], axis=0, keepdims=True)
            gmb = gm.astype(BF)
            parts.append(gmb)
            gn[s] += dot_nt(gmb, wm[:, cols])
        for k in range(window + 1):
            small_r[8 + k : 9 + k, cols] = sums[k]
        stage_out(0, dot(nt[...], jnp.concatenate(parts, axis=0)), gm_h.at[:, cols])
        return 0

    lax.fori_loop(0, xbc // BW, mixed_body, 0)
    for s in range(seqs):
        gn[s] += dot_nt(grl[s], ws3)

    def token_body(i, sums):
        for s in range(seqs):
            rows = ds(i * 16, 16)
            v = tok[s, rows, :].astype(F32)
            inv = lax.rsqrt(jnp.mean(v * v, axis=-1, keepdims=True) + EPSILON)
            unit = v * inv
            gr = gn[s, rows, :]
            sums = sums + jnp.sum(gr * unit, axis=0, keepdims=True)
            q = gr * gain
            back = inv * (q - unit * jnp.mean(q * unit, axis=-1, keepdims=True))
            tg_r[s, rows, :] = (cot[s, rows, :].astype(F32) + back).astype(BF)
        return sums

    small_r[6:7, 0:dm] = lax.fori_loop(
        0, length // 16, token_body, jnp.zeros((1, dm), F32)
    )

    @pl.when(has_next)
    def _():
        halo_copy.wait_send()

    def drain(c, _):
        @pl.when(has_next)
        def _():
            pltpu.make_async_remote_copy(
                src_ref=out_f.at[c], dst_ref=in_f.at[c], send_sem=fs_s.at[c],
                recv_sem=fs_r.at[c], device_id=nxt, device_id_type=MESH,
            ).wait_send()

        @pl.when(has_prev)
        def _():
            pltpu.make_async_remote_copy(
                src_ref=out_b.at[c], dst_ref=in_b.at[c], send_sem=bs_s.at[c],
                recv_sem=bs_r.at[c], device_id=prv, device_id_type=MESH,
            ).wait_send()

        return 0

    lax.fori_loop(0, nchunk, drain, 0)

    def drain_halo(b, _):
        @pl.when(has_prev)
        def _():
            gh_copy(b).wait_send()

        return 0

    lax.fori_loop(0, xbc // BW, drain_halo, 0)


def on_device(nctx, *args):
    tokens, norm_gain, wg, wm, ws, conv_w, conv_b, sb, lr, sk, gg, wo, cot = args
    seqs, length, dm = tokens.shape
    di = wg.shape[1]
    xbc = wm.shape[1]
    heads = ws.shape[1]
    nst = (xbc - di) // 2
    nchunk = di // LN
    hw = 16
    vm = pltpu.VMEM
    any_spec = pl.BlockSpec(memory_space=pl.ANY)
    vm_spec = pl.BlockSpec(memory_space=vm)
    dma = pltpu.SemaphoreType.DMA
    out = pl.pallas_call(
        functools.partial(layer_kernel, nctx),
        out_shape=(
            jax.ShapeDtypeStruct(tokens.shape, BF),
            jax.ShapeDtypeStruct(tokens.shape, BF),
            jax.ShapeDtypeStruct((di, dm), F32),
            jax.ShapeDtypeStruct((dm, di), F32),
            jax.ShapeDtypeStruct((dm, xbc), F32),
            jax.ShapeDtypeStruct((16, xbc), F32),
            jax.ShapeDtypeStruct((dm, LN), F32),
        ),
        in_specs=[any_spec, vm_spec, any_spec, any_spec] + [vm_spec] * 7 + [any_spec] * 2,
        out_specs=(vm_spec, vm_spec, any_spec, any_spec, any_spec, vm_spec, vm_spec),
        scratch_shapes=[
            vm((seqs, length, dm), BF),
            vm((seqs, length, dm), BF),
            vm((dm, di), BF),
            vm((dm, xbc), BF),
            vm((di, dm), BF),
            vm((seqs, hw, dm), BF),
            vm((seqs, hw + length, dm), BF),
            vm((dm, seqs * length), BF),
            vm((seqs, hw + length, xbc), BF),
            vm((seqs, length, xbc), F32),
            vm((seqs, length, di), BF),
            vm((seqs, length, di), BF),
            vm((seqs, length, di), F32),
            vm((seqs, length, di), F32),
            vm((seqs, length + 8, xbc), F32),
            vm((seqs, length, di), BF),
            vm((seqs, length, di), BF),
            vm((seqs, length, di), BF),
            vm((di, seqs * length), BF),
            vm((seqs, length, LN), F32),
            vm((seqs, length, LN), F32),
            vm((seqs, length, dm), F32),
            vm((nchunk, seqs, nst, LN), F32),
            vm((nchunk, seqs, nst, LN), F32),
            vm((nchunk, seqs, nst, LN), F32),
            vm((nchunk, seqs, nst, LN), BF),
            vm((nchunk, seqs, nst, LN), BF),
            vm((seqs, length, LN), F32),
            vm((seqs, length, LN), F32),
            vm((seqs, length, LN), F32),
            vm((seqs, LN, length), F32),
            vm((seqs, length, LN), BF),
            vm((seqs, length, LN), BF),
            vm((seqs, length, LN), BF),
            vm((seqs, 8, di), F32),
            vm((seqs, length, nst), BF),
            vm((seqs, length, nst), BF),
            vm((seqs, nst, length), BF),
            vm((seqs, nst, length), BF),
            vm((seqs, length, length), F32),
            vm((seqs, length, length), F32),
            vm((seqs, length, length), F32),
            vm((LN, di), BF),
            vm((2, length, length), BF),
            vm((seqs, length, nst), F32),
            vm((seqs, length, nst), F32),
            vm((seqs, length, LN), F32),
            vm((seqs, length, LN), F32),
            vm((seqs, 8, LN), F32),
            vm((8, di), F32),
            vm((2, dm, BW), F32),
            dma((5,)), dma, dma((2,)), dma, dma,
            dma((nchunk,)), dma((nchunk,)), dma((nchunk,)), dma((nchunk,)),
            dma((xbc // BW,)), dma((xbc // BW,)),
        ],
        compiler_params=pltpu.CompilerParams(
            collective_id=0, has_side_effects=True, vmem_limit_bytes=62 * 1024 * 1024
        ),
    )(*args)
    res, tg, g_out, g_gate, g_mixer, small, stepg = out
    both = ("seq", "ctx")
    g_out, g_gate, g_mixer, small, stepg = lax.psum(
        (g_out, g_gate, g_mixer, small, stepg), both
    )
    return (
        res, tg, small[6, :dm], g_gate, g_mixer, stepg[:, :heads], small[8:12], small[1],
        small[3, :heads], small[4, :heads], small[5, :heads], small[0, :di], g_out,
    )


def solution(mesh):
    tok = P("seq", "ctx", None)
    return jax.shard_map(
        functools.partial(on_device, mesh.shape["ctx"]),
        mesh=mesh,
        in_specs=(tok,) + (P(),) * 11 + (tok,),
        out_specs=(tok, tok) + (P(),) * 11,
        check_vma=False,
    )
```

time: 733 us -> 434 us (0.59); the launches traced: 724 us -> 433 us
  Pallas kernels: 0 us -> 132 us
  matrix products: 96.1 us -> 0 us
  other arithmetic: 93.1 us -> 0.01 us
  local copies, waits for them, and re-layouts: 111 us -> 22.2 us
  waiting for transfers between devices: 347 us -> 265 us
  blocking collectives: 56.8 us -> 0 us
    all_gather x2 -> x0, waiting for transfers between devices: 148 us -> none  [the longest x1 79 us: on_device(): shard_part = lax.all_gather(summary[None], 'ctx', axis=0, tiled=True)]
    pallas_call x0 -> x1, Pallas kernels: none -> 132 us  [on_device(): pl.pallas_call(functools.partial(layer_kernel, nctx), out_shape=(jax.Shap...]
    dot_general x24 -> x0, matrix products: 96.1 us -> none  [the longest x1 13.9 us: on_device(): jnp.einsum('spn,sun->sup', later_grad, inflow_wide, precision=HIGHEST)]
    psum x1, waiting for transfers between devices: 199 us -> 265 us  [on_device(): lax.psum((g_out, g_gate, g_mixer, small, stepg), both)]
    reduce_sum x14 -> x0, other arithmetic: 50.9 us -> none  [the longest x2 16.2 us: on_device(): jnp.sum(shard_part * heads_wide(weights, head_size)[..., None], axis=0)]
    psum x1 -> x0, blocking collectives: 44.2 us -> none  [on_device(): lax.psum((grad_norm_gain, grad_gate_weight, grad_mixer_weight, grad_step_...]
    mul x8 -> x0, local copies, waits for them, and re-layouts: 20 us -> none  [the longest x2 5.26 us: on_device(): grad_tail = head_sums(grad_scaled * signal * step_wide, head_count) * tail]
    reshape x5 -> x0, local copies, waits for them, and re-layouts: 15.6 us -> none  [the longest x2 7.1 us: heads_wide(): return jnp.repeat(value, head_size, axis=-1)]
  transfers between devices with their start and end apart: 5 -> 1, of which waited for: 3 -> 1; matrix products, arithmetic and copies ran while one was open for 17% -> 0% of each run, Pallas kernels for 0% -> 0%
where the time goes in v1:
time: 434 us; the launch traced here: 433 us
  waiting for transfers between devices  265 us (61%)
  Pallas kernels  132 us (30%)
  local copies, waits for them, and re-layouts  22.2 us (5%)
  between operations  14.1 us (3%)
    psum x1, waiting for transfers between devices, on_device(): lax.psum((g_out, g_gate, g_mixer, small, stepg), both)  265 us
    pallas_call x1, Pallas kernels, on_device(): pl.pallas_call(functools.partial(layer_kernel, nctx), out_shape=(jax.Shap...  132 us
    unnamed x19, local copies, waits for them, and re-layouts  15.3 us
  transfers between devices with their start and end apart: 1, of which 1 were waited for; matrix products, arithmetic and copies ran while one was open for 0% of the time, Pallas kernels for 0%

profile of v1, /device:TPU:0, one launch (start us, length us, event | category | flops | bytes accessed | tf_op | source)
XLA Modules:
  0.0 433.5 jit_solution(15073570919393001810)
XLA Ops:
  7.2 0.0 all-reduce.3.cloned.1.call-start
  7.2 1.6 copy.26.ws_r
  8.8 132.3 %shard_map.228 = (bf16[2,256,768]{2,1,0:T(8,128)(2,1)}, bf16[2,256,768]{2,1,0:T(8,128)(2,1)}, f32[1536,768]{1,0:T(8,128)}, f32[768,1536]{1,0:T(8,128)}, f32[768,...) custom-call(bf16[2,256,768]{2,1,0:T(8,128)(2,1)} %tok_h.1, f32[768]{0:T(1024)} %ng_r.1, ...), custom_call_target="tpu_custom_call" | custom-call | tf_op jit(solution)/shard_map/pallas_call | solution.py:672
  141.2 0.0 copy-start.1
  141.2 0.0 copy-start
  141.2 0.0 all-reduce.3.cloned.1.call-update
  141.2 264.8 %all-reduce.3.cloned.1.call-done = (f32[16,1792]{1,0:T(8,128)}, f32[768,1536]{1,0:T(8,128)}, f32[768,1792]{1,0:T(8,128)}, f32[768,128]{1,0:T(8,128)}, f32[1536,768]{1,0:T(8,128)}) async-done(((f32[16,1792]{1,0:T(8,128)}, f32[768,1536]{1,0:T(8,128)}, f32[768,1792]{1,0:T(8,128)}, f32[768,128]{1,0:T(8,128)}, f32[1536,768]{1,0:T(8,128)}), (f32[16,1792]{1,0:T(8,128)}, f32[768,1536]{1,0:T(8,128)}, ...) | async-done | bytes 15450128 | tf_op jit(solution)/shard_map/psum | solution.py:747
  406.0 1.3 slice_bitcast_fusion
  407.3 1.3 slice_reduce_fusion.2
  408.6 1.4 slice_reduce_fusion.1
  410.0 1.4 slice_reduce_fusion
  411.5 1.4 slice.34
  412.9 1.8 copy.27
  414.7 0.0 copy-done.1
  414.7 0.9 copy.38
  415.6 0.0 copy-done
  415.6 0.9 copy.39
  416.4 5.5 %copy.40 = f32[768,1536]{1,0:T(8,128)} copy(f32[768,1536]{1,0:T(8,128)} %get-tuple-element.64) | data formatting | bytes 9437184
  422.0 0.0 slice-done
  422.0 0.0 slice-done.1
  422.0 2.4 copy.41
  424.4 0.0 slice-done.2
  424.4 0.0 slice-done.3
  424.4 2.2 copy.42
  (6 shorter events, 0.0 us)
Async XLA Ops:
  7.2 398.8 %all-reduce.3.cloned.1.call-start = ((), (), s32[]{:S(2)}) async-start(), calls=%async_computation | async-start | bytes 30900224 | tf_op jit(solution)/shard_map/psum | solution.py:747
  141.2 273.5 %copy-start.1 = (bf16[2,256,768]{2,1,0:T(8,128)(2,1)S(1)}, bf16[2,256,768]{2,1,0:T(8,128)(2,1)}, u32[]{:S(2)}) copy-start(bf16[2,256,768]{2,1,0:T(8,128)(2,1)} %get-tuple-element.61) | copy-start | bytes 2359300
  141.2 274.4 %copy-start = (bf16[2,256,768]{2,1,0:T(8,128)(2,1)S(1)}, bf16[2,256,768]{2,1,0:T(8,128)(2,1)}, u32[]{:S(2)}) copy-start(bf16[2,256,768]{2,1,0:T(8,128)(2,1)} %get-tuple-element.62) | copy-start | bytes 2359300
  415.6 6.4 %slice-start = ((s8[5505024]{0:T(1024)(128)(4,1)}), s8[4194304]{0:T(1024)(128)(4,1)S(1)}, s32[]{:S(2)}) async-start(s8[5505024]{0:T(1024)(128)(4,1)} %bitcast.7), calls=%async_computation.1 | async-start | bytes 8388608
  416.4 5.5 %slice-start.1 = ((s8[5505024]{0:T(1024)(128)(4,1)}), s8[1310720]{0:T(1024)(128)(4,1)S(1)}, s32[]{:S(2)}) async-start(s8[5505024]{0:T(1024)(128)(4,1)} %bitcast.7), calls=%async_computation.2 | async-start | bytes 2621440
  416.4 8.0 %slice-start.2 = ((s8[4718592]{0:T(1024)(128)(4,1)}), s8[4194304]{0:T(1024)(128)(4,1)S(1)}, s32[]{:S(2)}) async-start(s8[4718592]{0:T(1024)(128)(4,1)} %bitcast.9), calls=%async_computation.3 | async-start | bytes 8388608
  422.0 2.5 slice-start.3
Sparse Core Ops, SparseCore 0:
  141.3 264.6 all-reduce.2

commit v2 on v1

--- a/solution.py
+++ b/solution.py
@@ -62,12 +62,12 @@
 def layer_kernel(
     nctx,
     tok_h, ng_r, wg_h, wm_h, ws_r, cw_r, cb_r, sb_r, lr_r, sk_r, gg_r, wo_h, cot_h,
-    res_r, tg_r, go_h, gw_h, gm_h, small_r, stepg_r,
+    res_h, tg_h, go_h, gw_h, gm_h, sm_h,
     tok, cot, wg, wm, wo, halo, ne, nt, ext, fil, drv, scl, y, z, big, gy, ggz, nrm, nrt,
-    acc_a, acc_b, gn, sum_s, out_f, in_f, out_b, in_b, sraw, st, cum, cum_t, pst, ptl, pdc,
-    dlast, infl, outf, inf_t, outf_t, sco, sco_t, gsc, xx, tri, ginf, gout, hs_d, hs_g, bdh,
-    skw, gstage,
-    in_sem, out_sem, st_sem, halo_s, halo_r, fs_s, fs_r, bs_s, bs_r, gh_s, gh_r,
+    acc_a, acc_b, gn, sum_s, in_f, out_b, in_b, sraw, st, cum, cum_t, pst, ptl, pdc,
+    dlast, infl, outf, inf_t, outf_t, sco, sco_t, xx, tri, hs_d, hs_g, bdh,
+    res_r, tok_sem, skw, sm, sk_row_r, bufs, ar_s, ar_r, loc_sem, ex_s, ex_r,
+    in_sem, halo_s, halo_r, fs_s, fs_r, bs_s, bs_r, gh_s, gh_r,
 ):
     seqs, length, dm = tok.shape
     di = wg.shape[1]
@@ -77,6 +77,7 @@
     nst = (xbc - di) // 2
     window = cw_r.shape[0] - 1
     nblk = di // BW
+    gsc, gout, ginf = sco, acc_a, acc_b
     nchunk = di // LN
     hw = 16
     seq = lax.axis_index("seq")
@@ -105,7 +106,28 @@
     for copy in loads:
         copy.start()
 
-    pl.semaphore_wait(barrier, has_prev.astype(jnp.int32) + has_next.astype(jnp.int32))
+    core = lax.rem(ctx, 2)
+
+    def flipped(index, mask):
+        bit = lax.rem(index // mask, 2)
+        return bit, index + mask - 2 * mask * bit
+
+    core_peer = (seq, flipped(ctx, 1)[1])
+    stages = []
+    for mask in (1 + core, 2 - core):
+        bit, other = flipped(seq, mask)
+        stages.append((bit, (other, ctx)))
+    mask = 2
+    while mask < nctx:
+        bit, other = flipped(ctx, mask)
+        stages.append((bit, (seq, other)))
+        mask *= 2
+    for _, peer in stages:
+        pl.semaphore_signal(barrier, inc=1, device_id=peer, device_id_type=MESH)
+    pl.semaphore_wait(
+        barrier, has_prev.astype(jnp.int32) + has_next.astype(jnp.int32) + len(stages)
+    )
+    stages, extras = stages[:4], stages[4:]
     loads[0].wait()
 
     halo_copy = pltpu.make_async_remote_copy(
@@ -252,7 +274,9 @@
         def _():
             for s in range(seqs):
                 row = dlast[s, 7:8, ds(c * LN, LN)]
-                out_buf[c, s] = (row * in_buf[c, s].astype(F32) + sum_s[c, s]).astype(out_buf.dtype)
+                out_buf[c, s] = (row * in_buf[c, s].astype(F32) + sum_s[c, s]).astype(
+                    out_buf.dtype
+                )
             copy.start()
 
     def relay_slot(slot, skew, *rest):
@@ -261,6 +285,21 @@
         @pl.when((c >= 0) & (c < nchunk))
         def _():
             relay(c, *rest)
+
+    SM_CONVB = 0
+    SM_GATE = SM_CONVB + xbc // LN
+    SM_NORM = SM_GATE + di // LN
+    SM_CONVW = SM_NORM + dm // LN
+    SM_HEADS = SM_CONVW + (window + 1) * (xbc // LN)
+    SM_STEP = -(-(SM_HEADS + 3) // 8) * 8
+    sm[...] = jnp.zeros_like(sm)
+
+    def small_one(row, value):
+        sm[row // 128, pl.ds(row % 128, 1), :] = value
+
+    def small_put(base, b, value):
+        small_one(base + 2 * b, value[:, :LN])
+        small_one(base + 2 * b + 1, value[:, LN:])
 
     half = length // 2
     d_r = lax.broadcasted_iota(jnp.int32, (half, half), 0)
@@ -304,7 +343,7 @@
     bskew = (3 * (nctx - 1 - ctx)) // 2
     slots = nchunk + (3 * (nctx - 1)) // 2
 
-    f_args = (in_f, out_f, (fs_s, fs_r), has_prev, has_next, nxt)
+    f_args = (in_f, sum_s, (fs_s, fs_r), has_prev, has_next, nxt)
     b_args = (in_b, out_b, (bs_s, bs_r), has_next, has_prev, prv)
 
     def forward_body(b, _):
@@ -326,6 +365,16 @@
         return 0
 
     lax.fori_loop(nchunk, slots, forward_rest, 0)
+
+    def sent_forward(c, _):
+        @pl.when(has_next)
+        def _():
+            pltpu.make_async_remote_copy(
+                src_ref=sum_s.at[c], dst_ref=in_f.at[c], send_sem=fs_s.at[c],
+                recv_sem=fs_r.at[c], device_id=nxt, device_id_type=MESH,
+            ).wait_send()
+
+        return 0
 
     acc_a[...] = jnp.zeros_like(acc_a)
     acc_b[...] = jnp.zeros_like(acc_b)
@@ -355,6 +404,7 @@
         inv_out.append(iv)
         mean_out.append(iv * jnp.sum(acc_b[s], axis=-1, keepdims=True) / di)
     gout[...] = jnp.zeros_like(gout)
+    lax.fori_loop(0, nchunk, sent_forward, 0)
 
     def grad_body(b, _):
         cols = ds(b * BW, BW)
@@ -383,7 +433,7 @@
             sum_s[2 * b + 1, s] = gp[:, LN:]
             phi, plo = split2(pr)
             gout[s] += dot_nt(whi, phi) + (dot_nt(wlo, phi) + dot_nt(whi, plo))
-        small_r[0:1, cols] = gg_sum
+        small_put(SM_GATE, b, gg_sum)
         return 0
 
     lax.fori_loop(0, nblk, grad_body, 0)
@@ -426,36 +476,173 @@
         z[s, :half, cols] = jnp.where(lane_low, lo[:half], lo[half:])
         z[s, half:, cols] = jnp.where(lane_low, hi[:half], hi[half:])
 
-    def stage_out(slot, value, dst):
-        gstage[slot] = value
-        copy = pltpu.make_async_copy(gstage.at[slot], dst, st_sem.at[slot])
-        copy.start()
+    sent = []
+    running = []
+
+    def wide(a_ref, b_ref, rows, cols):
+        t = dot(a_ref[rows, 0:length], b_ref[0, :, cols])
+        for s in range(1, seqs):
+            t = t + dot(a_ref[rows, s * length : (s + 1) * length], b_ref[s, :, cols])
+        return t
+
+    def from_out(i):
+        return lambda part, r0, n: wide(
+            nrt, cot, pl.ds(pl.multiple_of(i * dm + r0, 16), n),
+            pl.ds(pl.multiple_of(part * (dm // 2), LN), dm // 2),
+        )
+
+    def from_columns(ref, base, w):
+        return lambda part, r0, n: wide(
+            nt, ref, pl.ds(pl.multiple_of(r0, 16), n),
+            pl.ds(pl.multiple_of(base + part * w, LN), w),
+        )
+
+    def group_steps(g, produce, out_ref, row0, col0, part_cols):
+        sb, rb, rr, acc, rx = bufs[5 * g : 5 * g + 5]
+        total, w = sb.shape
+        kind = sb.dtype
+        tile = min(192, total // 2)
+
+        def place(off, n, part):
+            if part_cols:
+                return out_ref.at[
+                    pl.ds(pl.multiple_of(row0 + off, 8), n),
+                    pl.ds(pl.multiple_of(col0 + part * w, LN), w),
+                ]
+            return out_ref.at[pl.ds(pl.multiple_of(part * total + off, 8), n), :]
+
+        def copy_of(i, src, dst, peer):
+            copy = pltpu.make_async_remote_copy(
+                src_ref=src, dst_ref=dst, send_sem=ar_s.at[g, i], recv_sem=ar_r.at[g, i],
+                device_id=peer, device_id_type=MESH,
+            )
+            copy.start()
+            return copy
+
+        def rows_at(start, n):
+            return pl.ds(pl.multiple_of(start, 8), n)
+
+        def tiles(count, body):
+            if count == 1:
+                body(0)
+            else:
+                lax.fori_loop(0, count, lambda i, _: (body(i), 0)[1], 0)
+
+        def give(i):
+            sb[rows_at(i * tile, tile), :] = produce(1 - core, i * tile, tile).astype(kind)
+
+        tiles(total // tile, give)
+        copy = copy_of(0, sb, rb, core_peer)
+        yield
         copy.wait()
-
-    def backward_body(b, _):
-        cols = ds(b * BW, BW)
-        relay_slot(2 * b, bskew, *b_args)
-        both = jnp.concatenate([ggz[s, :, cols] for s in range(seqs)], axis=0)
-        stage_out(0, dot(nt[...], both), gw_h.at[:, cols])
-        rows = jnp.concatenate([cot[s] for s in range(seqs)], axis=0)
-        t = dot(nrt[cols, :], rows)
-        for i in range(dm // BW):
-            gstage[1, i * BW : (i + 1) * BW] = t[:, i * BW : (i + 1) * BW]
-        for i in range(dm // BW):
-            copy = pltpu.make_async_copy(
-                gstage.at[1, pl.ds(i * BW, BW)], go_h.at[cols, pl.ds(i * BW, BW)],
-                st_sem.at[1],
+        bit, peer = stages[0]
+        n = total // 2
+
+        def own(i, start):
+            r0 = start + i * tile
+            return produce(core, r0, tile) + rb[rows_at(r0, tile), :].astype(F32)
+
+        def give_half(i):
+            sb[rows_at(i * tile, tile), :] = own(i, (1 - bit) * n).astype(kind)
+
+        def keep_half(i):
+            acc[rows_at(i * tile, tile), :] = own(i, bit * n)
+
+        tiles(n // tile, give_half)
+        copy = copy_of(1, sb.at[pl.ds(0, n)], rr.at[pl.ds(0, n)], peer)
+        tiles(n // tile, keep_half)
+        first = copy
+        if not extras:
+            sent.append(first)
+        yield
+        base, at, off = 0, 0, bit * n
+        offs = [off]
+        for k in range(1, len(stages)):
+            copy.wait_recv()
+            bit, peer = stages[k]
+            n //= 2
+            nbase = base + 2 * n
+            r_give = (1 - bit) * n
+            r_keep = bit * n
+            sb[nbase : nbase + n, :] = (
+                acc[rows_at(at + r_give, n), :]
+                + rr[rows_at(base + r_give, n), :].astype(F32)
+            ).astype(kind)
+            copy = copy_of(k + 1, sb.at[pl.ds(nbase, n)], rr.at[pl.ds(nbase, n)], peer)
+            sent.append(copy)
+            acc[rows_at(at + r_keep, n), :] += rr[rows_at(base + r_keep, n), :].astype(F32)
+            base, at, off = nbase, at + r_keep, off + r_keep
+            offs.append(off)
+            yield
+        copy.wait_recv()
+        value = acc[rows_at(at, n), :] + rr[base : base + n, :].astype(F32)
+        if extras:
+            first.wait_send()
+        for e, (_, peer) in enumerate(extras):
+            mine = value.astype(kind)
+            sb[e * n : (e + 1) * n, :] = mine
+            copy = pltpu.make_async_remote_copy(
+                src_ref=sb.at[pl.ds(e * n, n)], dst_ref=rx.at[e], send_sem=ex_s.at[g, e],
+                recv_sem=ex_r.at[g, e], device_id=peer, device_id_type=MESH,
             )
             copy.start()
             copy.wait()
+            value = mine.astype(F32) + rx[e].astype(F32)
+        done = total - n
+        sb[done:, :] = value.astype(kind)
+        k = len(stages) - 1
+        here = place(offs[k], n, core)
+        local = pltpu.make_async_copy(sb.at[pl.ds(done, n)], here, loc_sem.at[g])
+        local.start()
+        copy = copy_of(5, sb.at[pl.ds(done, n)], here, stages[k][1])
+        sent.append(copy)
+        yield
+        local.wait()
+        for k in range(len(stages) - 2, -1, -1):
+            copy.wait_recv()
+            n *= 2
+            here = place(offs[k], n, core)
+            copy = copy_of(8 - k, here, here, stages[k][1])
+            sent.append(copy)
+            yield
+        copy.wait_recv()
+        here = place(0, total, core)
+        copy = copy_of(9, here, here, core_peer)
+        sent.append(copy)
+        yield
+        copy.wait_recv()
+
+    wide_w = dm // 2
+    groups = [
+        (0, from_out(0), go_h, 0, 0, True),
+        (1, from_out(1), go_h, dm, 0, True),
+        (2, from_columns(ggz, 0, wide_w), gw_h, 0, 0, True),
+        (3, from_columns(ggz, dm, wide_w), gw_h, 0, dm, True),
+        (4, from_columns(nrm, 0, wide_w), gm_h, 0, 0, True),
+        (5, from_columns(nrm, dm, wide_w), gm_h, 0, dm, True),
+        (6, from_columns(ggz, 0, LN), gm_h, 0, di, True),
+        (7, lambda part, r0, n: sm[part, pl.ds(pl.multiple_of(r0, 8), n), :], sm_h, 0, 0, False),
+    ]
+
+    def service(new=()):
+        for steps in list(running):
+            if next(steps, running) is running:
+                running.remove(steps)
+        for g in new:
+            steps = group_steps(*groups[g])
+            next(steps)
+            running.append(steps)
+
+    def backward_body(j, _):
+        relay_slot(j, bskew, *b_args)
         for s in range(seqs):
-            pair_backward(2 * b, s)
-        relay_slot(2 * b + 1, bskew, *b_args)
-        for s in range(seqs):
-            pair_backward(2 * b + 1, s)
-        return 0
-
-    lax.fori_loop(0, nblk, backward_body, 0)
+            pair_backward(j, s)
+        return 0
+
+    new = [[0], [1], [2], [3], [], []]
+    for i in range(nblk):
+        service(new[i])
+        lax.fori_loop(2 * i, 2 * i + 2, backward_body, 0)
 
     for s in range(seqs):
         for i in range(dm // BW):
@@ -463,12 +650,16 @@
             pj = dot(nrm[s], wo[:, cols])
             res_r[s, :, cols] = (tok[s, :, cols].astype(F32) + pj).astype(BF)
             gn[s, :, cols] = dot_nt(ggz[s], wg[cols, :])
+    res_copy = pltpu.make_async_copy(res_r, res_h, tok_sem.at[0])
+    res_copy.start()
+    service()
 
     def backward_rest(slot, _):
         relay_slot(slot, bskew, *b_args)
         return 0
 
     lax.fori_loop(nchunk, slots, backward_rest, 0)
+    service()
 
     ginf[...] = jnp.zeros_like(ginf)
     hs_d[...] = jnp.zeros_like(hs_d)
@@ -533,8 +724,8 @@
             gf = ga * (sg * (1.0 + f * (1.0 - sg)))
             big[s, 0:length, cols] = gf
             cb_sum = cb_sum + jnp.sum(gf, axis=0, keepdims=True)
-        small_r[1:2, cols] = cb_sum
-        small_r[2:3, cols] = sk_sum
+        small_put(SM_CONVB, b, cb_sum)
+        sk_row_r[0:1, cols] = sk_sum
 
         @pl.when(has_prev)
         def _():
@@ -542,7 +733,9 @@
 
         return 0
 
-    lax.fori_loop(0, nblk, last_body, 0)
+    for i in range(0, nblk, 2):
+        lax.fori_loop(i, i + 2, last_body, 0)
+        service()
 
     cb_sum = jnp.zeros((1, BW), F32)
     for s in range(seqs):
@@ -550,7 +743,7 @@
         gi = ginf[s] + dot(gst_bf, outf[s])
         go = gout[s] + dot(gst_bf.T, infl[s])
         cb_sum = cb_sum + finish_block(nblk, s, jnp.concatenate([gi, go], axis=1))
-    small_r[1:2, di:] = cb_sum
+    small_put(SM_CONVB, nblk, cb_sum)
 
     @pl.when(has_prev)
     def _():
@@ -568,13 +761,22 @@
         graw = gst * sigmoid(sraw[s] + bias3)
         gsb = gsb + jnp.sum(graw, axis=0, keepdims=True)
         grl.append(jnp.where(lane128 < heads, graw, 0.0).astype(BF))
-    small_r[3:4, 0:LN] = gsb
-    small_r[4:5, 0:LN] = rates3 * glr
-    sk_h = head_sum3(jnp.broadcast_to(small_r[2:3, :di], (8, di)), xx[...])
-    small_r[5:6, 0:LN] = sk_h[0:1]
-    stepg_r[...] = dot(nt[...], jnp.concatenate(grl, axis=0))
-
-    def mixed_body(b, _):
+    sk_h = head_sum3(jnp.broadcast_to(sk_row_r[0:1, :], (8, di)), xx[...])
+    small_one(SM_HEADS, gsb)
+    small_one(SM_HEADS + 1, rates3 * glr)
+    small_one(SM_HEADS + 2, sk_h[0:1])
+    stepg = dot(grl[0].T, ne[0, hw:, :])
+    for s in range(1, seqs):
+        stepg = stepg + dot(grl[s].T, ne[s, hw:, :])
+    for i in range(dm // LN):
+        row = SM_STEP + 24 * i
+        for lo, hi in ((row, min(row + 24, 128)), (max(row, 128), row + 24)):
+            if lo < hi:
+                sm[lo // 128, lo % 128 : lo % 128 + hi - lo, :] = stepg[
+                    lo - row : hi - row, i * LN : (i + 1) * LN
+                ]
+
+    def mixed_body(b):
         cols = ds(b * BW, BW)
 
         @pl.when(has_next)
@@ -598,13 +800,29 @@
             parts.append(gmb)
             gn[s] += dot_nt(gmb, wm[:, cols])
         for k in range(window + 1):
-            small_r[8 + k : 9 + k, cols] = sums[k]
-        stage_out(0, dot(nt[...], jnp.concatenate(parts, axis=0)), gm_h.at[:, cols])
-        return 0
-
-    lax.fori_loop(0, xbc // BW, mixed_body, 0)
+            small_put(SM_CONVW + k * (xbc // LN), b, sums[k])
+        return parts
+
+    def mixed_loop(b, _):
+        cols = ds(b * BW, BW)
+        for s, part in enumerate(mixed_body(b)):
+            nrm[s, :, cols] = part
+        return 0
+
+    lax.fori_loop(0, 3, mixed_loop, 0)
+    service([4])
+    lax.fori_loop(3, 6, mixed_loop, 0)
+    service([5])
+    for s, part in enumerate(mixed_body(6)):
+        ggz[s, :, 0:BW] = part
+    service([6])
     for s in range(seqs):
         gn[s] += dot_nt(grl[s], ws3)
+    service()
+
+    @pl.when(has_next)
+    def _():
+        halo_copy.wait_send()
 
     def token_body(i, sums):
         for s in range(seqs):
@@ -616,25 +834,23 @@
             sums = sums + jnp.sum(gr * unit, axis=0, keepdims=True)
             q = gr * gain
             back = inv * (q - unit * jnp.mean(q * unit, axis=-1, keepdims=True))
-            tg_r[s, rows, :] = (cot[s, rows, :].astype(F32) + back).astype(BF)
+            tok[s, rows, :] = (cot[s, rows, :].astype(F32) + back).astype(BF)
         return sums
 
-    small_r[6:7, 0:dm] = lax.fori_loop(
-        0, length // 16, token_body, jnp.zeros((1, dm), F32)
-    )
-
-    @pl.when(has_next)
-    def _():
-        halo_copy.wait_send()
+    n_sum = lax.fori_loop(0, length // 16, token_body, jnp.zeros((1, dm), F32))
+    for i in range(dm // LN):
+        small_one(SM_NORM + i, n_sum[:, i * LN : (i + 1) * LN])
+    tg_copy = pltpu.make_async_copy(tok, tg_h, tok_sem.at[1])
+    tg_copy.start()
+    service([7])
+    while running:
+        service()
+    res_copy.wait()
+    tg_copy.wait()
+    for copy in sent:
+        copy.wait_send()
 
     def drain(c, _):
-        @pl.when(has_next)
-        def _():
-            pltpu.make_async_remote_copy(
-                src_ref=out_f.at[c], dst_ref=in_f.at[c], send_sem=fs_s.at[c],
-                recv_sem=fs_r.at[c], device_id=nxt, device_id_type=MESH,
-            ).wait_send()
-
         @pl.when(has_prev)
         def _():
             pltpu.make_async_remote_copy(
@@ -669,19 +885,23 @@
     any_spec = pl.BlockSpec(memory_space=pl.ANY)
     vm_spec = pl.BlockSpec(memory_space=vm)
     dma = pltpu.SemaphoreType.DMA
+    extras = max(1, (nctx // 16).bit_length())
+    bufs = []
+    for rows, w, kind in [(dm, dm // 2, BF)] * 6 + [(dm, LN, BF), (128, LN, F32)]:
+        bufs += [vm((rows, w), kind)] * 3 + [vm((rows // 2, w), F32)]
+        bufs += [vm((extras, rows // 16, w), kind) if nctx > 8 else vm((1, 16, LN), kind)]
     out = pl.pallas_call(
         functools.partial(layer_kernel, nctx),
         out_shape=(
             jax.ShapeDtypeStruct(tokens.shape, BF),
             jax.ShapeDtypeStruct(tokens.shape, BF),
-            jax.ShapeDtypeStruct((di, dm), F32),
-            jax.ShapeDtypeStruct((dm, di), F32),
-            jax.ShapeDtypeStruct((dm, xbc), F32),
-            jax.ShapeDtypeStruct((16, xbc), F32),
-            jax.ShapeDtypeStruct((dm, LN), F32),
+            jax.ShapeDtypeStruct((di, dm), BF),
+            jax.ShapeDtypeStruct((dm, di), BF),
+            jax.ShapeDtypeStruct((dm, xbc), BF),
+            jax.ShapeDtypeStruct((256, LN), F32),
         ),
         in_specs=[any_spec, vm_spec, any_spec, any_spec] + [vm_spec] * 7 + [any_spec] * 2,
-        out_specs=(vm_spec, vm_spec, any_spec, any_spec, any_spec, vm_spec, vm_spec),
+        out_specs=(any_spec,) * 6,
         scratch_shapes=[
             vm((seqs, length, dm), BF),
             vm((seqs, length, dm), BF),
@@ -707,7 +927,6 @@
             vm((seqs, length, dm), F32),
             vm((nchunk, seqs, nst, LN), F32),
             vm((nchunk, seqs, nst, LN), F32),
-            vm((nchunk, seqs, nst, LN), F32),
             vm((nchunk, seqs, nst, LN), BF),
             vm((nchunk, seqs, nst, LN), BF),
             vm((seqs, length, LN), F32),
@@ -724,32 +943,40 @@
             vm((seqs, nst, length), BF),
             vm((seqs, length, length), F32),
             vm((seqs, length, length), F32),
-            vm((seqs, length, length), F32),
             vm((LN, di), BF),
             vm((2, length, length), BF),
-            vm((seqs, length, nst), F32),
-            vm((seqs, length, nst), F32),
             vm((seqs, length, LN), F32),
             vm((seqs, length, LN), F32),
             vm((seqs, 8, LN), F32),
+            vm((seqs, length, dm), BF),
+            dma((2,)),
             vm((8, di), F32),
-            vm((2, dm, BW), F32),
-            dma((5,)), dma, dma((2,)), dma, dma,
+            vm((2, 128, LN), F32),
+            vm((8, di), F32),
+            bufs,
+            dma((8, 10)), dma((8, 10)), dma((8,)), dma((8, extras)), dma((8, extras)),
+            dma((5,)), dma, dma,
             dma((nchunk,)), dma((nchunk,)), dma((nchunk,)), dma((nchunk,)),
             dma((xbc // BW,)), dma((xbc // BW,)),
         ],
         compiler_params=pltpu.CompilerParams(
-            collective_id=0, has_side_effects=True, vmem_limit_bytes=62 * 1024 * 1024
+            collective_id=0, has_side_effects=True, vmem_limit_bytes=65200 * 1024
         ),
     )(*args)
-    res, tg, g_out, g_gate, g_mixer, small, stepg = out
-    both = ("seq", "ctx")
-    g_out, g_gate, g_mixer, small, stepg = lax.psum(
-        (g_out, g_gate, g_mixer, small, stepg), both
-    )
+    res, tg, g_out, g_gate, g_mixer, small = out
+    gate0 = xbc // LN
+    norm0 = gate0 + di // LN
+    convw0 = norm0 + dm // LN
+    taps = conv_w.shape[0]
+    heads0 = convw0 + taps * (xbc // LN)
+    step0 = -(-(heads0 + 3) // 8) * 8
+    step = small[step0 : step0 + heads * (dm // LN)].reshape(dm // LN, heads, LN)
     return (
-        res, tg, small[6, :dm], g_gate, g_mixer, stepg[:, :heads], small[8:12], small[1],
-        small[3, :heads], small[4, :heads], small[5, :heads], small[0, :di], g_out,
+        res, tg, small[norm0:convw0].reshape(dm), g_gate.astype(F32), g_mixer.astype(F32),
+        step.transpose(0, 2, 1).reshape(dm, heads),
+        small[convw0:heads0].reshape(taps, xbc), small[:gate0].reshape(xbc),
+        small[heads0, :heads], small[heads0 + 1, :heads], small[heads0 + 2, :heads],
+        small[gate0:norm0].reshape(di), g_out.astype(F32),
     )
 
 

time: 434 us -> 217 us (0.50)
  waiting for transfers between devices: 265 us -> 0 us
  Pallas kernels: 132 us -> 198 us
  local copies, waits for them, and re-layouts: 22.2 us -> 7.65 us
  between operations: 14.1 us -> 0.67 us
  other arithmetic: 0.01 us -> 10 us
    psum x1 -> x0, waiting for transfers between devices: 265 us -> none  [on_device(): lax.psum((g_out, g_gate, g_mixer, small, stepg), both)]
    pallas_call x1, Pallas kernels: 132 us -> 198 us  [on_device(): pl.pallas_call(functools.partial(layer_kernel, nctx), out_shape=(jax.Shap...]
    unnamed x19 -> x14, local copies, waits for them, and re-layouts: 15.3 us -> 4.01 us
    convert_element_type x0 -> x3, other arithmetic: none -> 10 us  [the longest x1 4.65 us: on_device(): g_gate.astype(F32)]
    slice x4 -> x2, local copies, waits for them, and re-layouts: 5.63 us -> 0.01 us  [the longest x1 0.01 us: on_device(): step = small[step0:step0 + heads * (dm // LN)].reshape(dm // LN, heads, LN)]
  transfers between devices with their start and end apart: 1 -> 0, of which waited for: 1 -> 0; matrix products, arithmetic and copies ran while one was open for 0% -> 0% of each run, Pallas kernels for 0% -> 0%
where the time goes in v2:
time: 217 us
  Pallas kernels  198 us (91%)
  other arithmetic  10 us (5%)
  local copies, waits for them, and re-layouts  7.65 us (4%)
    pallas_call x1, Pallas kernels, on_device(): pl.pallas_call(functools.partial(layer_kernel, nctx), out_shape=(jax.Shap...  198 us
    convert_element_type x1, other arithmetic, on_device(): g_gate.astype(F32)  4.65 us

profile of v2, /device:TPU:0, one launch (start us, length us, event | category | flops | bytes accessed | tf_op | source)
XLA Modules:
  0.0 216.8 jit_solution(8826771209874597917)
XLA Ops:
  0.6 1.6 copy.28.ws_r
  2.2 198.5 %shard_map.228 = (bf16[2,256,768]{2,1,0:T(8,128)(2,1)}, bf16[2,256,768]{2,1,0:T(8,128)(2,1)}, bf16[1536,768]{1,0:T(8,128)(2,1)}, bf16[768,1536]{1,0:T(8,128)(2,1...) custom-call(bf16[2,256,768]{2,1,0:T(8,128)(2,1)} %tok_h.1, f32[768]{0:T(1024)} %ng_r.1, bf16[768,1536]{1,0:T(8,128)(2,1)} %wg_h.1, ...), custom_call_target="tpu_custom_call" | custom-call | tf_op jit(solution)/shard_map/pallas_call | solution.py:893
  200.7 1.3 slice_bitcast_fusion.2
  202.0 0.0 copy-start
  202.0 4.6 %convert_element_type.9 = f32[768,1536]{1,0:T(8,128)} convert(bf16[768,1536]{1,0:T(8,128)(2,1)} %get-tuple-element.22) | non-fusion elementwise | flops 1179648 | bytes 7077888 | tf_op jit(solution)/shard_map/convert_element_type | solution.py:975
  206.6 0.0 copy-done
  206.6 0.0 copy-start.4
  206.6 0.0 copy-start.1
  206.6 2.8 %convert_element_type.10 = f32[768,1792]{1,0:T(8,128)} convert(bf16[768,1792]{1,0:T(8,128)(2,1)S(1)} %copy-done) | non-fusion elementwise | flops 1376256 | bytes 8257536 | tf_op jit(solution)/shard_map/convert_element_type | solution.py:975
  209.5 0.0 copy-done.4
  209.5 0.6 copy.32
  210.2 0.6 reshape.47
  210.8 0.6 slice_bitcast_fusion.1
  211.4 0.5 slice_bitcast_fusion.3
  211.9 0.6 slice_bitcast_fusion
  212.5 0.0 copy-done.1
  212.5 0.0 copy-start.3
  212.5 0.0 copy-start.2
  212.5 2.5 %convert_element_type.11 = f32[1536,768]{1,0:T(8,128)} convert(bf16[1536,768]{1,0:T(8,128)(2,1)S(1)} %copy-done.1) | non-fusion elementwise | flops 1179648 | bytes 7077888 | tf_op jit(solution)/shard_map/convert_element_type | solution.py:979
  215.1 0.0 copy-done.3
  215.1 0.9 copy.35
  215.9 0.0 copy-done.2
  215.9 0.9 copy.36
  (3 shorter events, 0.0 us)
Async XLA Ops:
  202.0 4.7 %copy-start = (bf16[768,1792]{1,0:T(8,128)(2,1)S(1)}, bf16[768,1792]{1,0:T(8,128)(2,1)}, u32[]{:S(2)}) copy-start(bf16[768,1792]{1,0:T(8,128)(2,1)} %get-tuple-element.23) | copy-start | bytes 8257540
  206.6 2.9 %copy-start.4 = (f32[256,128]{1,0:T(8,128)S(1)}, f32[256,128]{1,0:T(8,128)}, u32[]{:S(2)}) copy-start(f32[256,128]{1,0:T(8,128)} %get-tuple-element.21) | copy-start | bytes 393220
  206.6 5.9 %copy-start.1 = (bf16[1536,768]{1,0:T(8,128)(2,1)S(1)}, bf16[1536,768]{1,0:T(8,128)(2,1)}, u32[]{:S(2)}) copy-start(bf16[1536,768]{1,0:T(8,128)(2,1)} %get-tuple-element.24) | copy-start | bytes 7077892
  212.5 2.6 %copy-start.3 = (bf16[2,256,768]{2,1,0:T(8,128)(2,1)S(1)}, bf16[2,256,768]{2,1,0:T(8,128)(2,1)}, u32[]{:S(2)}) copy-start(bf16[2,256,768]{2,1,0:T(8,128)(2,1)} %get-tuple-element.41) | copy-start | bytes 2359300
  212.5 3.4 %copy-start.2 = (bf16[2,256,768]{2,1,0:T(8,128)(2,1)S(1)}, bf16[2,256,768]{2,1,0:T(8,128)(2,1)}, u32[]{:S(2)}) copy-start(bf16[2,256,768]{2,1,0:T(8,128)(2,1)} %get-tuple-element.42) | copy-start | bytes 2359300

commit v3 on v2

--- a/solution.py
+++ b/solution.py
@@ -13,6 +13,27 @@
 EPSILON = 1e-05
 BW = 256
 LN = 128
+SKEW = 3
+PLAN = (
+    (0, 1, 2, 0, 1, 2, 3),
+    (0,),
+    (3, 1),
+    (),
+    (),
+    (2, 0),
+    (3,),
+    (1, 0, 2),
+    (3,),
+    (1,),
+    (0,),
+    (),
+    (2, 0, 4, 3),
+    (4, 0, 1, 5),
+    (0, 2, 6, 5, 3, 4, 1, 6, 2),
+    (),
+    (5, 3, 7, 4, 7, 1, 6, 1, 4, 2, 5, 2, 3, 4, 7, 6, 3, 5, 4, 7, 6, 5, 4, 7, 6, 4, 5, 7, 6,
+    5, 7, 6, 5, 6, 7, 7),
+)
 
 
 def dot(a, b):
@@ -117,17 +138,19 @@
     for mask in (1 + core, 2 - core):
         bit, other = flipped(seq, mask)
         stages.append((bit, (other, ctx)))
-    mask = 2
+    in_row = lax.rem(ctx // 2, 4)
+    row_peers = [(seq, ctx + 2 * (lax.rem(in_row + d, 4) - in_row)) for d in (1, 2, 3)]
+    extras = []
+    mask = 8
     while mask < nctx:
-        bit, other = flipped(ctx, mask)
-        stages.append((bit, (seq, other)))
+        extras.append((seq, flipped(ctx, mask)[1]))
         mask *= 2
-    for _, peer in stages:
+    peers = [peer for _, peer in stages] + row_peers + extras
+    for peer in peers:
         pl.semaphore_signal(barrier, inc=1, device_id=peer, device_id_type=MESH)
     pl.semaphore_wait(
-        barrier, has_prev.astype(jnp.int32) + has_next.astype(jnp.int32) + len(stages)
+        barrier, has_prev.astype(jnp.int32) + has_next.astype(jnp.int32) + len(peers)
     )
-    stages, extras = stages[:4], stages[4:]
     loads[0].wait()
 
     halo_copy = pltpu.make_async_remote_copy(
@@ -242,9 +265,61 @@
         sco[s] = dot_nt(o_bf, i_bf)
         sco_t[s] = dot_nt(i_bf, o_bf)
 
-    def signal_body(b, _):
-        cols = ds(b * BW, BW)
-        for s in range(seqs):
+    def forward_copy(q):
+        return pltpu.make_async_remote_copy(
+            src_ref=sum_s.at[q], dst_ref=in_f.at[q], send_sem=fs_s.at[q],
+            recv_sem=fs_r.at[q], device_id=nxt, device_id_type=MESH,
+        )
+
+    def backward_copy(q):
+        return pltpu.make_async_remote_copy(
+            src_ref=out_b.at[q], dst_ref=in_b.at[q], send_sem=bs_s.at[q],
+            recv_sem=bs_r.at[q], device_id=prv, device_id_type=MESH,
+        )
+
+    f_skew = SKEW * ctx
+    b_skew = SKEW * (nctx - 1 - ctx)
+    f_slots = seqs * nchunk + SKEW * (nctx - 1)
+    b_slots = seqs * nblk + SKEW * (nctx - 1)
+
+    def forward_slot(slot):
+        q = slot - f_skew
+
+        @pl.when((q >= 0) & (q < seqs * nchunk))
+        def _():
+            @pl.when(has_prev)
+            def _():
+                forward_copy(q).wait_recv()
+
+            @pl.when(has_next)
+            def _():
+                row = dlast[q // nchunk, 7:8, ds(lax.rem(q, nchunk) * LN, LN)]
+                sum_s[q] = row * in_f[q] + sum_s[q]
+                forward_copy(q).start()
+
+    def backward_slot(slot):
+        q = slot - b_skew
+
+        @pl.when((q >= 0) & (q < seqs * nblk))
+        def _():
+            @pl.when(has_next)
+            def _():
+                backward_copy(q).wait_recv()
+
+            @pl.when(has_prev)
+            def _():
+                row = dlast[q // nblk, 7:8, ds(lax.rem(q, nblk) * BW, BW)]
+                add = jnp.concatenate([sum_s[2 * q], sum_s[2 * q + 1]], axis=1)
+                out_b[q] = (row * in_b[q].astype(F32) + add).astype(BF)
+                backward_copy(q).start()
+
+    def slots_alone(one, first, last):
+        lax.fori_loop(first, last, lambda t, _: (one(t), 0)[1], 0)
+
+    for s in range(seqs):
+
+        def signal_body(b, _, s=s):
+            cols = ds(b * BW, BW)
             f = filter_block(b, s)
             sig = f * sigmoid(f)
             x = xx[:, cols]
@@ -254,37 +329,12 @@
             scl[s, :, cols] = sc
             y[s, :, cols] = skw[0:1, cols] * sig
             summ = dot(inf_t[s], sc)
-            sum_s[2 * b, s] = summ[:, :LN]
-            sum_s[2 * b + 1, s] = summ[:, LN:]
-        return 0
-
-    lax.fori_loop(0, nblk, signal_body, 0)
-
-    def relay(c, in_buf, out_buf, sems, has_in, has_out, to):
-        copy = pltpu.make_async_remote_copy(
-            src_ref=out_buf.at[c], dst_ref=in_buf.at[c], send_sem=sems[0].at[c],
-            recv_sem=sems[1].at[c], device_id=to, device_id_type=MESH,
-        )
-
-        @pl.when(has_in)
-        def _():
-            copy.wait_recv()
-
-        @pl.when(has_out)
-        def _():
-            for s in range(seqs):
-                row = dlast[s, 7:8, ds(c * LN, LN)]
-                out_buf[c, s] = (row * in_buf[c, s].astype(F32) + sum_s[c, s]).astype(
-                    out_buf.dtype
-                )
-            copy.start()
-
-    def relay_slot(slot, skew, *rest):
-        c = slot - skew
-
-        @pl.when((c >= 0) & (c < nchunk))
-        def _():
-            relay(c, *rest)
+            sum_s[s * nchunk + 2 * b] = summ[:, :LN]
+            sum_s[s * nchunk + 2 * b + 1] = summ[:, LN:]
+            forward_slot(s * nblk + b)
+            return 0
+
+        lax.fori_loop(0, nblk, signal_body, 0)
 
     SM_CONVB = 0
     SM_GATE = SM_CONVB + xbc // LN
@@ -339,104 +389,112 @@
     loads[3].wait()
     loads[4].wait()
 
-    fskew = (3 * ctx) // 2
-    bskew = (3 * (nctx - 1 - ctx)) // 2
-    slots = nchunk + (3 * (nctx - 1)) // 2
-
-    f_args = (in_f, sum_s, (fs_s, fs_r), has_prev, has_next, nxt)
-    b_args = (in_b, out_b, (bs_s, bs_r), has_next, has_prev, prv)
-
-    def forward_body(b, _):
-        cols = ds(b * BW, BW)
-        relay_slot(2 * b, fskew, *f_args)
-        for s in range(seqs):
+    for s in range(seqs):
+
+        def forward_body(b, _, s=s):
+            cols = ds(b * BW, BW)
             big[s, 0:length, cols] = dot_nt(cot[s], wo[cols, :])
             pair_forward(2 * b, s)
-        relay_slot(2 * b + 1, fskew, *f_args)
-        for s in range(seqs):
             z[s, :, cols] = dot(ne[s, hw : hw + length, :], wg[:, cols])
             pair_forward(2 * b + 1, s)
-        return 0
-
-    lax.fori_loop(0, nblk, forward_body, 0)
-
-    def forward_rest(slot, _):
-        relay_slot(slot, fskew, *f_args)
-        return 0
-
-    lax.fori_loop(nchunk, slots, forward_rest, 0)
-
-    def sent_forward(c, _):
-        @pl.when(has_next)
-        def _():
-            pltpu.make_async_remote_copy(
-                src_ref=sum_s.at[c], dst_ref=in_f.at[c], send_sem=fs_s.at[c],
-                recv_sem=fs_r.at[c], device_id=nxt, device_id_type=MESH,
-            ).wait_send()
-
-        return 0
+            forward_slot((seqs + s) * nblk + b)
+            return 0
+
+        lax.fori_loop(0, nblk, forward_body, 0)
 
     acc_a[...] = jnp.zeros_like(acc_a)
     acc_b[...] = jnp.zeros_like(acc_b)
 
-    def gate_body(b, _):
+    def prior_of(s, b):
+        return jnp.concatenate(
+            [in_f[s * nchunk + 2 * b], in_f[s * nchunk + 2 * b + 1]], axis=1
+        )
+
+    def gate_block(b, s):
         cols = ds(b * BW, BW)
-        for s in range(seqs):
-            pr = jnp.concatenate([in_f[2 * b, s], in_f[2 * b + 1, s]], axis=1)
-            phi, plo = split2(pr)
-            out = (dot(outf[s], phi) + dot(outf[s], plo)) * dot(pdc[s], xx[:, cols])
-            yy = y[s, :, cols] + out
-            y[s, :, cols] = yy
-            zz = z[s, :, cols]
-            gated = yy * (zz * sigmoid(zz))
-            q = big[s, 0:length, cols] * gg_r[cols].reshape(1, BW)
-            a = gated * gated
-            c = q * gated
-            acc_a[s] += a[:, :LN] + a[:, LN:]
-            acc_b[s] += c[:, :LN] + c[:, LN:]
+        phi, plo = split2(prior_of(s, b))
+        out = (dot(outf[s], phi) + dot(outf[s], plo)) * dot(pdc[s], xx[:, cols])
+        yy = y[s, :, cols] + out
+        y[s, :, cols] = yy
+        zz = z[s, :, cols]
+        gated = yy * (zz * sigmoid(zz))
+        q = big[s, 0:length, cols] * gg_r[cols].reshape(1, BW)
+        a = gated * gated
+        c = q * gated
+        acc_a[s] += a[:, :LN] + a[:, LN:]
+        acc_b[s] += c[:, :LN] + c[:, LN:]
+
+    def grad_block(b, s, iv, mean):
+        cols = ds(b * BW, BW)
+        yy = y[s, :, cols]
+        zz = z[s, :, cols]
+        sg = sigmoid(zz)
+        act = zz * sg
+        unit = (yy * act) * iv
+        gain_row = gg_r[cols].reshape(1, BW)
+        g = big[s, 0:length, cols]
+        no = (unit * gain_row).astype(BF)
+        nrm[s, :, cols] = no
+        nrt[cols, s * length : (s + 1) * length] = no.T
+        sk_row_r[1 + s : 2 + s, cols] = jnp.sum(g * unit, axis=0, keepdims=True)
+        gr = iv * (g * gain_row - unit * mean)
+        gyb = (gr * act).astype(BF)
+        gy[s, :, cols] = gyb
+        ggz[s, :, cols] = (gr * yy * (sg * (1.0 + zz * (1.0 - sg)))).astype(BF)
+        w = gyb.astype(F32) * dot(pdc[s], xx[:, cols])
+        whi, wlo = split2(w)
+        gp = dot(outf_t[s], whi) + dot(outf_t[s], wlo)
+        sum_s[s * nchunk + 2 * b] = gp[:, :LN]
+        sum_s[s * nchunk + 2 * b + 1] = gp[:, LN:]
+        phi, plo = split2(prior_of(s, b))
+        gout[s] += dot_nt(whi, phi) + (dot_nt(wlo, phi) + dot_nt(whi, plo))
+
+    first_done = f_slots - nchunk * (seqs - 1)
+    slots_alone(forward_slot, seqs * nchunk, first_done)
+    for s in range(seqs):
+        slot0 = first_done + s * nchunk
+
+        def passing(i, s=s, slot0=slot0):
+            if s < seqs - 1:
+                forward_slot(slot0 + i)
+            else:
+                backward_slot(i)
+
+        def gate_body(b, _, s=s, passing=passing):
+            gate_block(b, s)
+            passing(b)
+            return 0
+
+        lax.fori_loop(0, nblk, gate_body, 0)
+        iv = lax.rsqrt(jnp.sum(acc_a[s], axis=-1, keepdims=True) / di + EPSILON)
+        mean = iv * jnp.sum(acc_b[s], axis=-1, keepdims=True) / di
+        gout[s] = jnp.zeros_like(gout[s])
+
+        def sent_forward(c, _, s=s):
+            @pl.when(has_next)
+            def _():
+                forward_copy(s * nchunk + c).wait_send()
+
+            return 0
+
+        lax.fori_loop(0, nchunk, sent_forward, 0)
+
+        def grad_body(b, _, s=s, iv=iv, mean=mean, passing=passing):
+            grad_block(b, s, iv, mean)
+            passing(nblk + b)
+            return 0
+
+        lax.fori_loop(0, nblk, grad_body, 0)
+
+    def gate_gain_body(b, _):
+        cols = ds(b * BW, BW)
+        total = sk_row_r[1:2, cols]
+        for s in range(1, seqs):
+            total = total + sk_row_r[1 + s : 2 + s, cols]
+        small_put(SM_GATE, b, total)
         return 0
 
-    lax.fori_loop(0, nblk, gate_body, 0)
-
-    inv_out, mean_out = [], []
-    for s in range(seqs):
-        iv = lax.rsqrt(jnp.sum(acc_a[s], axis=-1, keepdims=True) / di + EPSILON)
-        inv_out.append(iv)
-        mean_out.append(iv * jnp.sum(acc_b[s], axis=-1, keepdims=True) / di)
-    gout[...] = jnp.zeros_like(gout)
-    lax.fori_loop(0, nchunk, sent_forward, 0)
-
-    def grad_body(b, _):
-        cols = ds(b * BW, BW)
-        gg_sum = jnp.zeros((1, BW), F32)
-        for s in range(seqs):
-            yy = y[s, :, cols]
-            zz = z[s, :, cols]
-            sg = sigmoid(zz)
-            act = zz * sg
-            unit = (yy * act) * inv_out[s]
-            gain_row = gg_r[cols].reshape(1, BW)
-            g = big[s, 0:length, cols]
-            no = (unit * gain_row).astype(BF)
-            nrm[s, :, cols] = no
-            nrt[cols, s * length : (s + 1) * length] = no.T
-            gg_sum = gg_sum + jnp.sum(g * unit, axis=0, keepdims=True)
-            gr = inv_out[s] * (g * gain_row - unit * mean_out[s])
-            gyb = (gr * act).astype(BF)
-            gy[s, :, cols] = gyb
-            ggz[s, :, cols] = (gr * yy * (sg * (1.0 + zz * (1.0 - sg)))).astype(BF)
-            w = gyb.astype(F32) * dot(pdc[s], xx[:, cols])
-            whi, wlo = split2(w)
-            pr = jnp.concatenate([in_f[2 * b, s], in_f[2 * b + 1, s]], axis=1)
-            gp = dot(outf_t[s], whi) + dot(outf_t[s], wlo)
-            sum_s[2 * b, s] = gp[:, :LN]
-            sum_s[2 * b + 1, s] = gp[:, LN:]
-            phi, plo = split2(pr)
-            gout[s] += dot_nt(whi, phi) + (dot_nt(wlo, phi) + dot_nt(whi, plo))
-        small_put(SM_GATE, b, gg_sum)
-        return 0
-
-    lax.fori_loop(0, nblk, grad_body, 0)
+    lax.fori_loop(0, nblk, gate_gain_body, 0)
 
     gsc[...] = jnp.zeros_like(gsc)
 
@@ -477,7 +535,6 @@
         z[s, half:, cols] = jnp.where(lane_low, hi[:half], hi[half:])
 
     sent = []
-    running = []
 
     def wide(a_ref, b_ref, rows, cols):
         t = dot(a_ref[rows, 0:length], b_ref[0, :, cols])
@@ -517,6 +574,7 @@
                 device_id=peer, device_id_type=MESH,
             )
             copy.start()
+            sent.append(copy)
             return copy
 
         def rows_at(start, n):
@@ -533,6 +591,7 @@
 
         tiles(total // tile, give)
         copy = copy_of(0, sb, rb, core_peer)
+        sent.pop()
         yield
         copy.wait()
         bit, peer = stages[0]
@@ -551,34 +610,46 @@
         tiles(n // tile, give_half)
         copy = copy_of(1, sb.at[pl.ds(0, n)], rr.at[pl.ds(0, n)], peer)
         tiles(n // tile, keep_half)
-        first = copy
-        if not extras:
-            sent.append(first)
+        first_copy = copy
+        if extras:
+            sent.pop()
         yield
-        base, at, off = 0, 0, bit * n
-        offs = [off]
-        for k in range(1, len(stages)):
+        copy.wait_recv()
+        off1 = bit * n
+        bit, peer = stages[1]
+        base, n = n, n // 2
+        gone, kept = (1 - bit) * n, bit * n
+        sb[base : base + n, :] = (
+            acc[rows_at(gone, n), :] + rr[rows_at(gone, n), :].astype(F32)
+        ).astype(kind)
+        copy = copy_of(2, sb.at[pl.ds(base, n)], rr.at[pl.ds(base, n)], peer)
+        acc[rows_at(kept, n), :] += rr[rows_at(kept, n), :].astype(F32)
+        yield
+        copy.wait_recv()
+        off2 = off1 + kept
+        first, base, n = base, base + n, n // 4
+        copies = []
+        for d in (2, 1, 3):
+            at = lax.rem(in_row + d, 4) * n
+            here = base + (d - 1) * n
+            sb[here : here + n, :] = (
+                acc[rows_at(kept + at, n), :] + rr[rows_at(first + at, n), :].astype(F32)
+            ).astype(kind)
+            copies.append(
+                copy_of(
+                    2 + d, sb.at[pl.ds(here, n)], rr.at[pl.ds(here, n)], row_peers[d - 1]
+                )
+            )
+        yield
+        at = in_row * n
+        value = acc[rows_at(kept + at, n), :] + rr[rows_at(first + at, n), :].astype(F32)
+        for copy in copies:
             copy.wait_recv()
-            bit, peer = stages[k]
-            n //= 2
-            nbase = base + 2 * n
-            r_give = (1 - bit) * n
-            r_keep = bit * n
-            sb[nbase : nbase + n, :] = (
-                acc[rows_at(at + r_give, n), :]
-                + rr[rows_at(base + r_give, n), :].astype(F32)
-            ).astype(kind)
-            copy = copy_of(k + 1, sb.at[pl.ds(nbase, n)], rr.at[pl.ds(nbase, n)], peer)
-            sent.append(copy)
-            acc[rows_at(at + r_keep, n), :] += rr[rows_at(base + r_keep, n), :].astype(F32)
-            base, at, off = nbase, at + r_keep, off + r_keep
-            offs.append(off)
-            yield
-        copy.wait_recv()
-        value = acc[rows_at(at, n), :] + rr[base : base + n, :].astype(F32)
+        for d in range(3):
+            value = value + rr[base + d * n : base + (d + 1) * n, :].astype(F32)
         if extras:
-            first.wait_send()
-        for e, (_, peer) in enumerate(extras):
+            first_copy.wait_send()
+        for e, peer in enumerate(extras):
             mine = value.astype(kind)
             sb[e * n : (e + 1) * n, :] = mine
             copy = pltpu.make_async_remote_copy(
@@ -590,27 +661,25 @@
             value = mine.astype(F32) + rx[e].astype(F32)
         done = total - n
         sb[done:, :] = value.astype(kind)
-        k = len(stages) - 1
-        here = place(offs[k], n, core)
+        here = place(off2 + at, n, core)
+        copies = [
+            copy_of(5 + d, sb.at[pl.ds(done, n)], here, row_peers[d - 1]) for d in (2, 1, 3)
+        ]
         local = pltpu.make_async_copy(sb.at[pl.ds(done, n)], here, loc_sem.at[g])
         local.start()
-        copy = copy_of(5, sb.at[pl.ds(done, n)], here, stages[k][1])
-        sent.append(copy)
         yield
+        for copy in copies:
+            copy.wait_recv()
         local.wait()
-        for k in range(len(stages) - 2, -1, -1):
+        for i, off, n, peer in (
+            (9, off2, total // 4, stages[1][1]),
+            (10, off1, total // 2, stages[0][1]),
+            (11, 0, total, core_peer),
+        ):
+            here = place(off, n, core)
+            copy = copy_of(i, here, here, peer)
+            yield
             copy.wait_recv()
-            n *= 2
-            here = place(offs[k], n, core)
-            copy = copy_of(8 - k, here, here, stages[k][1])
-            sent.append(copy)
-            yield
-        copy.wait_recv()
-        here = place(0, total, core)
-        copy = copy_of(9, here, here, core_peer)
-        sent.append(copy)
-        yield
-        copy.wait_recv()
 
     wide_w = dm // 2
     groups = [
@@ -624,42 +693,41 @@
         (7, lambda part, r0, n: sm[part, pl.ds(pl.multiple_of(r0, 8), n), :], sm_h, 0, 0, False),
     ]
 
-    def service(new=()):
-        for steps in list(running):
-            if next(steps, running) is running:
-                running.remove(steps)
-        for g in new:
-            steps = group_steps(*groups[g])
-            next(steps)
-            running.append(steps)
-
-    def backward_body(j, _):
-        relay_slot(j, bskew, *b_args)
-        for s in range(seqs):
-            pair_backward(j, s)
-        return 0
-
-    new = [[0], [1], [2], [3], [], []]
-    for i in range(nblk):
-        service(new[i])
-        lax.fori_loop(2 * i, 2 * i + 2, backward_body, 0)
-
+    plan = list(PLAN)
+    live = {}
+
+    def service(last=False):
+        todo = [g for part in plan for g in part] if last else plan.pop(0)
+        for g in todo:
+            if g not in live:
+                live[g] = group_steps(*groups[g])
+            next(live[g], None)
+
+    for i in range(seqs * nblk // 2):
+        s, b0 = (2 * i) // nblk, (2 * i) % nblk
+
+        def backward_body(b, _, s=s):
+            pair_backward(2 * b, s)
+            pair_backward(2 * b + 1, s)
+            backward_slot((seqs + s) * nblk + b)
+            return 0
+
+        service()
+        lax.fori_loop(b0, b0 + 2, backward_body, 0)
+
+    slot = 2 * seqs * nblk
     for s in range(seqs):
         for i in range(dm // BW):
             cols = slice(i * BW, (i + 1) * BW)
             pj = dot(nrm[s], wo[:, cols])
             res_r[s, :, cols] = (tok[s, :, cols].astype(F32) + pj).astype(BF)
             gn[s, :, cols] = dot_nt(ggz[s], wg[cols, :])
+            backward_slot(slot)
+            slot += 1
+        service()
     res_copy = pltpu.make_async_copy(res_r, res_h, tok_sem.at[0])
     res_copy.start()
-    service()
-
-    def backward_rest(slot, _):
-        relay_slot(slot, bskew, *b_args)
-        return 0
-
-    lax.fori_loop(nchunk, slots, backward_rest, 0)
-    service()
+    slots_alone(backward_slot, slot, b_slots)
 
     ginf[...] = jnp.zeros_like(ginf)
     hs_d[...] = jnp.zeros_like(hs_d)
@@ -699,8 +767,8 @@
         sk_sum = jnp.zeros((1, BW), F32)
         x = xx[:, cols]
         for s in range(seqs):
-            lt = jnp.concatenate([in_b[2 * b, s], in_b[2 * b + 1, s]], axis=1)
-            pr = jnp.concatenate([in_f[2 * b, s], in_f[2 * b + 1, s]], axis=1)
+            lt = in_b[s * nblk + b]
+            pr = prior_of(s, b)
             f = fil[s, :, cols]
             sg = sigmoid(f)
             sig = f * sg
@@ -809,13 +877,14 @@
             nrm[s, :, cols] = part
         return 0
 
+    service()
     lax.fori_loop(0, 3, mixed_loop, 0)
-    service([4])
+    service()
     lax.fori_loop(3, 6, mixed_loop, 0)
-    service([5])
+    service()
     for s, part in enumerate(mixed_body(6)):
         ggz[s, :, 0:BW] = part
-    service([6])
+    service()
     for s in range(seqs):
         gn[s] += dot_nt(grl[s], ws3)
     service()
@@ -842,25 +911,20 @@
         small_one(SM_NORM + i, n_sum[:, i * LN : (i + 1) * LN])
     tg_copy = pltpu.make_async_copy(tok, tg_h, tok_sem.at[1])
     tg_copy.start()
-    service([7])
-    while running:
-        service()
+    service(last=True)
     res_copy.wait()
     tg_copy.wait()
     for copy in sent:
         copy.wait_send()
 
-    def drain(c, _):
+    def drain(q, _):
         @pl.when(has_prev)
         def _():
-            pltpu.make_async_remote_copy(
-                src_ref=out_b.at[c], dst_ref=in_b.at[c], send_sem=bs_s.at[c],
-                recv_sem=bs_r.at[c], device_id=prv, device_id_type=MESH,
-            ).wait_send()
+            backward_copy(q).wait_send()
 
         return 0
 
-    lax.fori_loop(0, nchunk, drain, 0)
+    lax.fori_loop(0, seqs * nblk, drain, 0)
 
     def drain_halo(b, _):
         @pl.when(has_prev)
@@ -880,6 +944,7 @@
     heads = ws.shape[1]
     nst = (xbc - di) // 2
     nchunk = di // LN
+    nblk = di // BW
     hw = 16
     vm = pltpu.VMEM
     any_spec = pl.BlockSpec(memory_space=pl.ANY)
@@ -925,10 +990,10 @@
             vm((seqs, length, LN), F32),
             vm((seqs, length, LN), F32),
             vm((seqs, length, dm), F32),
-            vm((nchunk, seqs, nst, LN), F32),
-            vm((nchunk, seqs, nst, LN), F32),
-            vm((nchunk, seqs, nst, LN), BF),
-            vm((nchunk, seqs, nst, LN), BF),
+            vm((seqs * nchunk, nst, LN), F32),
+            vm((seqs * nchunk, nst, LN), F32),
+            vm((seqs * nblk, nst, BW), BF),
+            vm((seqs * nblk, nst, BW), BF),
             vm((seqs, length, LN), F32),
             vm((seqs, length, LN), F32),
             vm((seqs, length, LN), F32),
@@ -954,9 +1019,9 @@
             vm((2, 128, LN), F32),
             vm((8, di), F32),
             bufs,
-            dma((8, 10)), dma((8, 10)), dma((8,)), dma((8, extras)), dma((8, extras)),
+            dma((8, 12)), dma((8, 12)), dma((8,)), dma((8, extras)), dma((8, extras)),
             dma((5,)), dma, dma,
-            dma((nchunk,)), dma((nchunk,)), dma((nchunk,)), dma((nchunk,)),
+            dma((seqs * nchunk,)), dma((seqs * nchunk,)), dma((seqs * nblk,)), dma((seqs * nblk,)),
             dma((xbc // BW,)), dma((xbc // BW,)),
         ],
         compiler_params=pltpu.CompilerParams(

time: 217 us -> 168 us (0.77)
  Pallas kernels: 198 us -> 150 us
    pallas_call x1, Pallas kernels: 198 us -> 150 us  [on_device(): pl.pallas_call(functools.partial(layer_kernel, nctx), out_shape=(jax.Shap...]
where the time goes in v3:
time: 168 us
  Pallas kernels  150 us (89%)
  other arithmetic  10 us (6%)
  local copies, waits for them, and re-layouts  7.65 us (5%)
    pallas_call x1, Pallas kernels, on_device(): pl.pallas_call(functools.partial(layer_kernel, nctx), out_shape=(jax.Shap...  150 us
    convert_element_type x1, other arithmetic, on_device(): g_gate.astype(F32)  4.65 us
    unnamed x14, local copies, waits for them, and re-layouts  4.01 us

profile of v3, /device:TPU:0, one launch (start us, length us, event | category | flops | bytes accessed | tf_op | source)
XLA Modules:
  0.0 168.2 jit_solution(5175990898250742497)
XLA Ops:
  0.6 1.6 copy.28.ws_r
  2.2 149.9 %shard_map.228 = (bf16[2,256,768]{2,1,0:T(8,128)(2,1)}, bf16[2,256,768]{2,1,0:T(8,128)(2,1)}, bf16[1536,768]{1,0:T(8,128)(2,1)}, bf16[768,1536]{1,0:T(8,128)(2,1...) custom-call(bf16[2,256,768]{2,1,0:T(8,128)(2,1)} %tok_h.1, f32[768]{0:T(1024)} %ng_r.1, bf16[768,1536]{1,0:T(8,128)(2,1)} %wg_h.1, ...), custom_call_target="tpu_custom_call" | custom-call | tf_op jit(solution)/shard_map/pallas_call | solution.py:958
  152.1 1.3 slice_bitcast_fusion.2
  153.4 0.0 copy-start
  153.4 4.6 %convert_element_type.9 = f32[768,1536]{1,0:T(8,128)} convert(bf16[768,1536]{1,0:T(8,128)(2,1)} %get-tuple-element.22) | non-fusion elementwise | flops 1179648 | bytes 7077888 | tf_op jit(solution)/shard_map/convert_element_type | solution.py:1040
  158.0 0.0 copy-done
  158.0 0.0 copy-start.4
  158.0 0.0 copy-start.1
  158.0 2.8 %convert_element_type.10 = f32[768,1792]{1,0:T(8,128)} convert(bf16[768,1792]{1,0:T(8,128)(2,1)S(1)} %copy-done) | non-fusion elementwise | flops 1376256 | bytes 8257536 | tf_op jit(solution)/shard_map/convert_element_type | solution.py:1040
  160.9 0.0 copy-done.4
  160.9 0.6 copy.32
  161.6 0.6 reshape.47
  162.2 0.6 slice_bitcast_fusion.1
  162.8 0.5 slice_bitcast_fusion.3
  163.3 0.6 slice_bitcast_fusion
  163.9 0.0 copy-done.1
  163.9 0.0 copy-start.3
  163.9 0.0 copy-start.2
  163.9 2.5 %convert_element_type.11 = f32[1536,768]{1,0:T(8,128)} convert(bf16[1536,768]{1,0:T(8,128)(2,1)S(1)} %copy-done.1) | non-fusion elementwise | flops 1179648 | bytes 7077888 | tf_op jit(solution)/shard_map/convert_element_type | solution.py:1044
  166.5 0.0 copy-done.3
  166.5 0.9 copy.35
  167.4 0.0 copy-done.2
  167.4 0.9 copy.36
  (3 shorter events, 0.0 us)
Async XLA Ops:
  153.4 4.7 %copy-start = (bf16[768,1792]{1,0:T(8,128)(2,1)S(1)}, bf16[768,1792]{1,0:T(8,128)(2,1)}, u32[]{:S(2)}) copy-start(bf16[768,1792]{1,0:T(8,128)(2,1)} %get-tuple-element.23) | copy-start | bytes 8257540
  158.0 2.9 %copy-start.4 = (f32[256,128]{1,0:T(8,128)S(1)}, f32[256,128]{1,0:T(8,128)}, u32[]{:S(2)}) copy-start(f32[256,128]{1,0:T(8,128)} %get-tuple-element.21) | copy-start | bytes 393220
  158.0 5.9 %copy-start.1 = (bf16[1536,768]{1,0:T(8,128)(2,1)S(1)}, bf16[1536,768]{1,0:T(8,128)(2,1)}, u32[]{:S(2)}) copy-start(bf16[1536,768]{1,0:T(8,128)(2,1)} %get-tuple-element.24) | copy-start | bytes 7077892
  163.9 2.6 %copy-start.3 = (bf16[2,256,768]{2,1,0:T(8,128)(2,1)S(1)}, bf16[2,256,768]{2,1,0:T(8,128)(2,1)}, u32[]{:S(2)}) copy-start(bf16[2,256,768]{2,1,0:T(8,128)(2,1)} %get-tuple-element.41) | copy-start | bytes 2359300
  163.9 3.4 %copy-start.2 = (bf16[2,256,768]{2,1,0:T(8,128)(2,1)S(1)}, bf16[2,256,768]{2,1,0:T(8,128)(2,1)}, u32[]{:S(2)}) copy-start(bf16[2,256,768]{2,1,0:T(8,128)(2,1)} %get-tuple-element.42) | copy-start | bytes 2359300

commit v4 on v3

--- a/solution.py
+++ b/solution.py
@@ -13,26 +13,27 @@
 EPSILON = 1e-05
 BW = 256
 LN = 128
-SKEW = 3
+SKEW = 2
 PLAN = (
-    (0, 1, 2, 0, 1, 2, 3),
+    (1, 0, 2, 1, 0, 2, 3),
+    (),
+    (1, 3),
     (0,),
-    (3, 1),
     (),
     (),
-    (2, 0),
-    (3,),
-    (1, 0, 2),
-    (3,),
+    (2, 1),
+    (3, 0),
+    (4, 1, 3, 2, 4, 0),
     (1,),
-    (0,),
+    (4, 5, 1, 3),
+    (6, 5, 4, 2, 6, 0),
+    (1,),
     (),
-    (2, 0, 4, 3),
-    (4, 0, 1, 5),
-    (0, 2, 6, 5, 3, 4, 1, 6, 2),
-    (),
-    (5, 3, 7, 4, 7, 1, 6, 1, 4, 2, 5, 2, 3, 4, 7, 6, 3, 5, 4, 7, 6, 5, 4, 7, 6, 4, 5, 7, 6,
-    5, 7, 6, 5, 6, 7, 7),
+    (3, 1),
+    (5, 6),
+    (4, 0),
+    (2, 7, 6, 7, 5, 4, 7, 2, 0, 3, 7, 0, 6, 5, 4, 6, 7, 3, 7, 5, 4, 4, 7, 6, 5, 2, 2, 6, 6,
+    7, 7, 3, 5, 5),
 )
 
 
@@ -93,7 +94,7 @@
     seqs, length, dm = tok.shape
     di = wg.shape[1]
     xbc = wm.shape[1]
-    heads = ws_r.shape[1]
+    heads = ws_r.shape[0]
     hp = di // heads
     nst = (xbc - di) // 2
     window = cw_r.shape[0] - 1
@@ -124,7 +125,7 @@
             ((tok_h, tok), (wm_h, wm), (cot_h, cot), (wo_h, wo), (wg_h, wg))
         )
     ]
-    for copy in loads:
+    for copy in loads[:2]:
         copy.start()
 
     core = lax.rem(ctx, 2)
@@ -148,33 +149,11 @@
     peers = [peer for _, peer in stages] + row_peers + extras
     for peer in peers:
         pl.semaphore_signal(barrier, inc=1, device_id=peer, device_id_type=MESH)
-    pl.semaphore_wait(
-        barrier, has_prev.astype(jnp.int32) + has_next.astype(jnp.int32) + len(peers)
-    )
-    loads[0].wait()
-
-    halo_copy = pltpu.make_async_remote_copy(
-        src_ref=tok.at[:, pl.ds(length - hw, hw), :], dst_ref=halo, send_sem=halo_s,
-        recv_sem=halo_r, device_id=nxt, device_id_type=MESH,
-    )
-
-    @pl.when(has_next)
-    def _():
-        halo_copy.start()
-
-    @pl.when(jnp.logical_not(has_prev))
-    def _():
-        halo[...] = jnp.zeros_like(halo)
-        in_f[...] = jnp.zeros_like(in_f)
-
-    @pl.when(jnp.logical_not(has_next))
-    def _():
-        in_b[...] = jnp.zeros_like(in_b)
-
     lane128 = lax.broadcasted_iota(jnp.int32, (1, LN), 1)
     r_i = lax.broadcasted_iota(jnp.int32, (LN, di), 0)
     c_i = lax.broadcasted_iota(jnp.int32, (LN, di), 1)
-    xx[...] = jnp.where((r_i % 32 == c_i // hp) & (r_i < 96), 1.0, 0.0).astype(BF)
+    first = jnp.bitwise_and(r_i, 31) * hp
+    xx[...] = jnp.where((c_i >= first) & (c_i < first + hp) & (r_i < 96), 1.0, 0.0).astype(BF)
     t_r = lax.broadcasted_iota(jnp.int32, (length, length), 0)
     t_c = lax.broadcasted_iota(jnp.int32, (length, length), 1)
     tri[0] = jnp.where(t_r >= t_c, 1.0, 0.0).astype(BF)
@@ -189,11 +168,36 @@
         r = rep.astype(BF)
         return (dot(hi, r) + dot(mid, r) + dot(lo, r))[0:1]
 
-    ws3 = dot(ws_r[...], rep.astype(BF)).astype(BF)
+    ws3 = dot(ws_r[...].T, rep.astype(BF)).astype(BF)
     bias3 = replicated(sb_r)
     rates3 = -jnp.exp(replicated(lr_r))
     sk8 = jnp.broadcast_to(replicated(sk_r), (8, LN))
     skw[...] = dot(pieces3(sk8), xx[...])
+
+    pl.semaphore_wait(
+        barrier, has_prev.astype(jnp.int32) + has_next.astype(jnp.int32) + len(peers)
+    )
+    loads[0].wait()
+    for copy in loads[2:]:
+        copy.start()
+
+    halo_copy = pltpu.make_async_remote_copy(
+        src_ref=tok.at[:, pl.ds(length - hw, hw), :], dst_ref=halo, send_sem=halo_s,
+        recv_sem=halo_r, device_id=nxt, device_id_type=MESH,
+    )
+
+    @pl.when(has_next)
+    def _():
+        halo_copy.start()
+
+    @pl.when(jnp.logical_not(has_prev))
+    def _():
+        halo[...] = jnp.zeros_like(halo)
+        in_f[...] = jnp.zeros_like(in_f)
+
+    @pl.when(jnp.logical_not(has_next))
+    def _():
+        in_b[...] = jnp.zeros_like(in_b)
 
     gain = ng_r[...].reshape(1, dm)
 
@@ -242,19 +246,19 @@
 
     def filter_block(b, s):
         cols = ds(b * BW, BW)
-        m = dot(ne[s], wm[:, cols]).astype(BF)
-        ext[s, :, cols] = m
-        m = m.astype(F32)
+        m_bf = dot(ne[s], wm[:, cols]).astype(BF)
+        m = m_bf.astype(F32)
         f = cb_r[cols].reshape(1, BW)
         for k in range(window + 1):
             shift = window - k
             moved = pltpu.roll(m, shift, 0) if shift else m
             f = f + cw_r[k : k + 1, cols] * moved[hw:]
+        return cols, m_bf, f
+
+    for s in range(seqs):
+        cols, m_bf, f = filter_block(nblk, s)
+        ext[s, :, cols] = m_bf
         fil[s, :, cols] = f
-        return f
-
-    for s in range(seqs):
-        f = filter_block(nblk, s)
         act = f * sigmoid(f)
         i_bf = act[:, :nst].astype(BF)
         o_bf = act[:, nst:].astype(BF)
@@ -318,23 +322,30 @@
 
     for s in range(seqs):
 
-        def signal_body(b, _, s=s):
-            cols = ds(b * BW, BW)
-            f = filter_block(b, s)
-            sig = f * sigmoid(f)
-            x = xx[:, cols]
-            dr = sig * dot(pst[s], x)
-            drv[s, :, cols] = dr.astype(BF)
-            sc = (dr * dot(ptl[s], x)).astype(BF)
-            scl[s, :, cols] = sc
-            y[s, :, cols] = skw[0:1, cols] * sig
-            summ = dot(inf_t[s], sc)
-            sum_s[s * nchunk + 2 * b] = summ[:, :LN]
-            sum_s[s * nchunk + 2 * b + 1] = summ[:, LN:]
-            forward_slot(s * nblk + b)
+        def signal_body(i, _, s=s):
+            made = []
+            for b in (2 * i, 2 * i + 1):
+                cols, m_bf, f = filter_block(b, s)
+                sig = f * sigmoid(f)
+                x = xx[:, cols]
+                dr = sig * dot(pst[s], x)
+                sc = (dr * dot(ptl[s], x)).astype(BF)
+                made.append(
+                    (b, cols, m_bf, f, skw[0:1, cols] * sig, dr.astype(BF), sc, dot(inf_t[s], sc))
+                )
+            for b, cols, m_bf, f, sk_sig, dr, sc, summ in made:
+                ext[s, :, cols] = m_bf
+                fil[s, :, cols] = f
+                y[s, :, cols] = sk_sig
+                drv[s, :, cols] = dr
+                scl[s, :, cols] = sc
+                sum_s[s * nchunk + 2 * b] = summ[:, :LN]
+                sum_s[s * nchunk + 2 * b + 1] = summ[:, LN:]
+            for slot in (2 * i, 2 * i + 1):
+                forward_slot(s * nblk + slot)
             return 0
 
-        lax.fori_loop(0, nblk, signal_body, 0)
+        lax.fori_loop(0, nblk // 2, signal_body, 0)
 
     SM_CONVB = 0
     SM_GATE = SM_CONVB + xbc // LN
@@ -382,8 +393,10 @@
             )
         lo = dot(jnp.concatenate(top, axis=0), d[:half])
         hi = dot(jnp.concatenate(bottom, axis=0), d)
-        y[s, :half, cols] += jnp.where(lane_low, lo[:half], lo[half:])
-        y[s, half:, cols] += jnp.where(lane_low, hi[:half], hi[half:])
+        return (
+            y[s, :half, cols] + jnp.where(lane_low, lo[:half], lo[half:]),
+            y[s, half:, cols] + jnp.where(lane_low, hi[:half], hi[half:]),
+        )
 
     loads[2].wait()
     loads[3].wait()
@@ -391,16 +404,29 @@
 
     for s in range(seqs):
 
-        def forward_body(b, _, s=s):
-            cols = ds(b * BW, BW)
-            big[s, 0:length, cols] = dot_nt(cot[s], wo[cols, :])
-            pair_forward(2 * b, s)
-            z[s, :, cols] = dot(ne[s, hw : hw + length, :], wg[:, cols])
-            pair_forward(2 * b + 1, s)
-            forward_slot((seqs + s) * nblk + b)
+        def forward_body(i, _, s=s):
+            made = []
+            for b in (2 * i, 2 * i + 1):
+                cols = ds(b * BW, BW)
+                made.append(
+                    (
+                        b, cols, dot_nt(cot[s], wo[cols, :]),
+                        dot(ne[s, hw : hw + length, :], wg[:, cols]),
+                        [pair_forward(2 * b + h, s) for h in range(2)],
+                    )
+                )
+            for b, cols, g, zz, pairs in made:
+                big[s, 0:length, cols] = g
+                z[s, :, cols] = zz
+                for h, (lo, hi) in enumerate(pairs):
+                    lanes = ds((2 * b + h) * LN, LN)
+                    y[s, :half, lanes] = lo
+                    y[s, half:, lanes] = hi
+            for slot in (2 * i, 2 * i + 1):
+                forward_slot((seqs + s) * nblk + slot)
             return 0
 
-        lax.fori_loop(0, nblk, forward_body, 0)
+        lax.fori_loop(0, nblk // 2, forward_body, 0)
 
     acc_a[...] = jnp.zeros_like(acc_a)
     acc_b[...] = jnp.zeros_like(acc_b)
@@ -410,44 +436,60 @@
             [in_f[s * nchunk + 2 * b], in_f[s * nchunk + 2 * b + 1]], axis=1
         )
 
-    def gate_block(b, s):
-        cols = ds(b * BW, BW)
-        phi, plo = split2(prior_of(s, b))
-        out = (dot(outf[s], phi) + dot(outf[s], plo)) * dot(pdc[s], xx[:, cols])
-        yy = y[s, :, cols] + out
-        y[s, :, cols] = yy
-        zz = z[s, :, cols]
-        gated = yy * (zz * sigmoid(zz))
-        q = big[s, 0:length, cols] * gg_r[cols].reshape(1, BW)
-        a = gated * gated
-        c = q * gated
-        acc_a[s] += a[:, :LN] + a[:, LN:]
-        acc_b[s] += c[:, :LN] + c[:, LN:]
-
-    def grad_block(b, s, iv, mean):
-        cols = ds(b * BW, BW)
-        yy = y[s, :, cols]
-        zz = z[s, :, cols]
-        sg = sigmoid(zz)
-        act = zz * sg
-        unit = (yy * act) * iv
-        gain_row = gg_r[cols].reshape(1, BW)
-        g = big[s, 0:length, cols]
-        no = (unit * gain_row).astype(BF)
-        nrm[s, :, cols] = no
-        nrt[cols, s * length : (s + 1) * length] = no.T
-        sk_row_r[1 + s : 2 + s, cols] = jnp.sum(g * unit, axis=0, keepdims=True)
-        gr = iv * (g * gain_row - unit * mean)
-        gyb = (gr * act).astype(BF)
-        gy[s, :, cols] = gyb
-        ggz[s, :, cols] = (gr * yy * (sg * (1.0 + zz * (1.0 - sg)))).astype(BF)
-        w = gyb.astype(F32) * dot(pdc[s], xx[:, cols])
-        whi, wlo = split2(w)
-        gp = dot(outf_t[s], whi) + dot(outf_t[s], wlo)
-        sum_s[s * nchunk + 2 * b] = gp[:, :LN]
-        sum_s[s * nchunk + 2 * b + 1] = gp[:, LN:]
-        phi, plo = split2(prior_of(s, b))
-        gout[s] += dot_nt(whi, phi) + (dot_nt(wlo, phi) + dot_nt(whi, plo))
+    def gate_blocks(blocks, s):
+        made = []
+        a_sum = c_sum = None
+        for b in blocks:
+            cols = ds(b * BW, BW)
+            phi, plo = split2(prior_of(s, b))
+            out = (dot(outf[s], phi) + dot(outf[s], plo)) * dot(pdc[s], xx[:, cols])
+            yy = y[s, :, cols] + out
+            zz = z[s, :, cols]
+            gated = yy * (zz * sigmoid(zz))
+            q = big[s, 0:length, cols] * gg_r[cols].reshape(1, BW)
+            a = gated * gated
+            c = q * gated
+            a, c = a[:, :LN] + a[:, LN:], c[:, :LN] + c[:, LN:]
+            a_sum, c_sum = (a, c) if a_sum is None else (a_sum + a, c_sum + c)
+            made.append((cols, yy))
+        for cols, yy in made:
+            y[s, :, cols] = yy
+        acc_a[s] += a_sum
+        acc_b[s] += c_sum
+
+    def grad_blocks(blocks, s, iv, mean):
+        made = []
+        g_out = None
+        for b in blocks:
+            cols = ds(b * BW, BW)
+            yy = y[s, :, cols]
+            zz = z[s, :, cols]
+            sg = sigmoid(zz)
+            act = zz * sg
+            unit = (yy * act) * iv
+            gain_row = gg_r[cols].reshape(1, BW)
+            g = big[s, 0:length, cols]
+            no = (unit * gain_row).astype(BF)
+            gain_sum = jnp.sum(g * unit, axis=0, keepdims=True)
+            gr = iv * (g * gain_row - unit * mean)
+            gyb = (gr * act).astype(BF)
+            gzb = (gr * yy * (sg * (1.0 + zz * (1.0 - sg)))).astype(BF)
+            w = gyb.astype(F32) * dot(pdc[s], xx[:, cols])
+            whi, wlo = split2(w)
+            gp = dot(outf_t[s], whi) + dot(outf_t[s], wlo)
+            phi, plo = split2(prior_of(s, b))
+            go = dot_nt(whi, phi) + (dot_nt(wlo, phi) + dot_nt(whi, plo))
+            g_out = go if g_out is None else g_out + go
+            made.append((b, cols, no, no.T, gain_sum, gyb, gzb, gp))
+        for b, cols, no, no_t, gain_sum, gyb, gzb, gp in made:
+            nrm[s, :, cols] = no
+            nrt[cols, s * length : (s + 1) * length] = no_t
+            sk_row_r[1 + s : 2 + s, cols] = gain_sum
+            gy[s, :, cols] = gyb
+            ggz[s, :, cols] = gzb
+            sum_s[s * nchunk + 2 * b] = gp[:, :LN]
+            sum_s[s * nchunk + 2 * b + 1] = gp[:, LN:]
+        gout[s] += g_out
 
     first_done = f_slots - nchunk * (seqs - 1)
     slots_alone(forward_slot, seqs * nchunk, first_done)
@@ -460,12 +502,13 @@
             else:
                 backward_slot(i)
 
-        def gate_body(b, _, s=s, passing=passing):
-            gate_block(b, s)
-            passing(b)
+        def gate_body(i, _, s=s, passing=passing):
+            gate_blocks((2 * i, 2 * i + 1), s)
+            passing(2 * i)
+            passing(2 * i + 1)
             return 0
 
-        lax.fori_loop(0, nblk, gate_body, 0)
+        lax.fori_loop(0, nblk // 2, gate_body, 0)
         iv = lax.rsqrt(jnp.sum(acc_a[s], axis=-1, keepdims=True) / di + EPSILON)
         mean = iv * jnp.sum(acc_b[s], axis=-1, keepdims=True) / di
         gout[s] = jnp.zeros_like(gout[s])
@@ -479,12 +522,13 @@
 
         lax.fori_loop(0, nchunk, sent_forward, 0)
 
-        def grad_body(b, _, s=s, iv=iv, mean=mean, passing=passing):
-            grad_block(b, s, iv, mean)
-            passing(nblk + b)
+        def grad_body(i, _, s=s, iv=iv, mean=mean, passing=passing):
+            grad_blocks((2 * i, 2 * i + 1), s, iv, mean)
+            passing(nblk + 2 * i)
+            passing(nblk + 2 * i + 1)
             return 0
 
-        lax.fori_loop(0, nblk, grad_body, 0)
+        lax.fori_loop(0, nblk // 2, grad_body, 0)
 
     def gate_gain_body(b, _):
         cols = ds(b * BW, BW)
@@ -526,13 +570,12 @@
             bottom.append((sco_t[s, half:, half:] * fc).astype(BF))
             p1, p2, p3 = m1[:, :half] * fa, m1[:, half:] * fb, m2 * fc
             t1, t2, t3 = (p1, p2, p3) if hh == 0 else (t1 + p1, t2 + p2, t3 + p3)
-        gsc[s, :half, :half] += t1
-        gsc[s, :half, half:] += t2
-        gsc[s, half:, half:] += t3
         lo = dot(jnp.concatenate(top, axis=0), g)
         hi = dot(jnp.concatenate(bottom, axis=0), g[half:])
-        z[s, :half, cols] = jnp.where(lane_low, lo[:half], lo[half:])
-        z[s, half:, cols] = jnp.where(lane_low, hi[:half], hi[half:])
+        return (
+            cols, (t1, t2, t3), jnp.where(lane_low, lo[:half], lo[half:]),
+            jnp.where(lane_low, hi[:half], hi[half:]),
+        )
 
     sent = []
 
@@ -558,15 +601,14 @@
         sb, rb, rr, acc, rx = bufs[5 * g : 5 * g + 5]
         total, w = sb.shape
         kind = sb.dtype
-        tile = min(192, total // 2)
-
-        def place(off, n, part):
+        tile = min(384, total // 2)
+
+        def place(part):
             if part_cols:
                 return out_ref.at[
-                    pl.ds(pl.multiple_of(row0 + off, 8), n),
-                    pl.ds(pl.multiple_of(col0 + part * w, LN), w),
+                    pl.ds(row0, total), pl.ds(pl.multiple_of(col0 + part * w, LN), w)
                 ]
-            return out_ref.at[pl.ds(pl.multiple_of(part * total + off, 8), n), :]
+            return out_ref.at[pl.ds(pl.multiple_of(part * total, 8), total), :]
 
         def copy_of(i, src, dst, peer):
             copy = pltpu.make_async_remote_copy(
@@ -659,27 +701,29 @@
             copy.start()
             copy.wait()
             value = mine.astype(F32) + rx[e].astype(F32)
-        done = total - n
-        sb[done:, :] = value.astype(kind)
-        here = place(off2 + at, n, core)
+        mine = rows_at(off2 + at, n)
+        rb[mine, :] = value.astype(kind)
         copies = [
-            copy_of(5 + d, sb.at[pl.ds(done, n)], here, row_peers[d - 1]) for d in (2, 1, 3)
+            copy_of(5 + d, rb.at[mine], rb.at[mine], row_peers[d - 1]) for d in (2, 1, 3)
         ]
-        local = pltpu.make_async_copy(sb.at[pl.ds(done, n)], here, loc_sem.at[g])
-        local.start()
         yield
         for copy in copies:
             copy.wait_recv()
-        local.wait()
         for i, off, n, peer in (
             (9, off2, total // 4, stages[1][1]),
             (10, off1, total // 2, stages[0][1]),
-            (11, 0, total, core_peer),
         ):
-            here = place(off, n, core)
+            here = rb.at[rows_at(off, n)]
             copy = copy_of(i, here, here, peer)
             yield
             copy.wait_recv()
+        here = place(core)
+        copy = copy_of(11, rb, here, core_peer)
+        local = pltpu.make_async_copy(rb, here, loc_sem.at[g])
+        local.start()
+        yield
+        copy.wait_recv()
+        local.wait()
 
     wide_w = dm // 2
     groups = [
@@ -687,9 +731,9 @@
         (1, from_out(1), go_h, dm, 0, True),
         (2, from_columns(ggz, 0, wide_w), gw_h, 0, 0, True),
         (3, from_columns(ggz, dm, wide_w), gw_h, 0, dm, True),
-        (4, from_columns(nrm, 0, wide_w), gm_h, 0, 0, True),
-        (5, from_columns(nrm, dm, wide_w), gm_h, 0, dm, True),
-        (6, from_columns(ggz, 0, LN), gm_h, 0, di, True),
+        (4, from_columns(gy, 0, wide_w), gm_h, 0, 0, True),
+        (5, from_columns(gy, dm, wide_w), gm_h, 0, dm, True),
+        (6, from_columns(drv, 0, LN), gm_h, 0, di, True),
         (7, lambda part, r0, n: sm[part, pl.ds(pl.multiple_of(r0, 8), n), :], sm_h, 0, 0, False),
     ]
 
@@ -704,30 +748,24 @@
             next(live[g], None)
 
     for i in range(seqs * nblk // 2):
-        s, b0 = (2 * i) // nblk, (2 * i) % nblk
+        s, i0 = (2 * i) // nblk, (2 * i) % nblk
 
         def backward_body(b, _, s=s):
-            pair_backward(2 * b, s)
-            pair_backward(2 * b + 1, s)
+            made = [pair_backward(2 * b + h, s) for h in range(2)]
+            t1, t2, t3 = (p + q for p, q in zip(made[0][1], made[1][1]))
+            gsc[s, :half, :half] += t1
+            gsc[s, :half, half:] += t2
+            gsc[s, half:, half:] += t3
+            for cols, _, lo, hi in made:
+                z[s, :half, cols] = lo
+                z[s, half:, cols] = hi
             backward_slot((seqs + s) * nblk + b)
             return 0
 
         service()
-        lax.fori_loop(b0, b0 + 2, backward_body, 0)
-
-    slot = 2 * seqs * nblk
-    for s in range(seqs):
-        for i in range(dm // BW):
-            cols = slice(i * BW, (i + 1) * BW)
-            pj = dot(nrm[s], wo[:, cols])
-            res_r[s, :, cols] = (tok[s, :, cols].astype(F32) + pj).astype(BF)
-            gn[s, :, cols] = dot_nt(ggz[s], wg[cols, :])
-            backward_slot(slot)
-            slot += 1
-        service()
-    res_copy = pltpu.make_async_copy(res_r, res_h, tok_sem.at[0])
-    res_copy.start()
-    slots_alone(backward_slot, slot, b_slots)
+        lax.fori_loop(i0, i0 + 2, backward_body, 0)
+    slots_alone(backward_slot, 2 * seqs * nblk, b_slots)
+    service()
 
     ginf[...] = jnp.zeros_like(ginf)
     hs_d[...] = jnp.zeros_like(hs_d)
@@ -801,9 +839,44 @@
 
         return 0
 
-    for i in range(0, nblk, 2):
-        lax.fori_loop(i, i + 2, last_body, 0)
-        service()
+    def mixed_body(b):
+        cols = ds(b * BW, BW)
+
+        @pl.when(has_next)
+        def _():
+            gh_copy(b).wait_recv()
+
+        parts = []
+        sums = [jnp.zeros((1, BW), F32) for _ in range(window + 1)]
+        for s in range(seqs):
+            gf = big[s, :, cols]
+            rows = gf.shape[0]
+            m = ext[s, :, cols].astype(F32)
+            gm = jnp.zeros((length, BW), F32)
+            for k in range(window + 1):
+                shift = window - k
+                moved = pltpu.roll(gf, rows - shift, 0) if shift else gf
+                gm = gm + cw_r[k : k + 1, cols] * moved[:length]
+                em = pltpu.roll(m, shift, 0) if shift else m
+                sums[k] = sums[k] + jnp.sum(gf[:length] * em[hw:], axis=0, keepdims=True)
+            parts.append(gm.astype(BF))
+        for k in range(window + 1):
+            small_put(SM_CONVW + k * (xbc // LN), b, sums[k])
+        return parts
+
+    def mixed_loop(b, _):
+        cols = ds(b * BW, BW)
+        for s, part in enumerate(mixed_body(b)):
+            gy[s, :, cols] = part
+        return 0
+
+    third = nblk // 2
+    lax.fori_loop(0, third, last_body, 0)
+    service()
+    lax.fori_loop(0, third, mixed_loop, 0)
+    service()
+    lax.fori_loop(third, nblk, last_body, 0)
+    service()
 
     cb_sum = jnp.zeros((1, BW), F32)
     for s in range(seqs):
@@ -816,6 +889,12 @@
     @pl.when(has_prev)
     def _():
         gh_copy(nblk).start()
+
+    lax.fori_loop(third, nblk, mixed_loop, 0)
+    service()
+    for s, part in enumerate(mixed_body(nblk)):
+        drv[s, :, 0:BW] = part
+    service()
 
     row_i = lax.broadcasted_iota(jnp.int32, (length, LN), 0)
     glr = jnp.zeros((1, LN), F32)
@@ -844,50 +923,25 @@
                     lo - row : hi - row, i * LN : (i + 1) * LN
                 ]
 
-    def mixed_body(b):
-        cols = ds(b * BW, BW)
-
-        @pl.when(has_next)
-        def _():
-            gh_copy(b).wait_recv()
-
-        parts = []
-        sums = [jnp.zeros((1, BW), F32) for _ in range(window + 1)]
-        for s in range(seqs):
-            gf = big[s, :, cols]
-            rows = gf.shape[0]
-            m = ext[s, :, cols].astype(F32)
-            gm = jnp.zeros((length, BW), F32)
-            for k in range(window + 1):
-                shift = window - k
-                moved = pltpu.roll(gf, rows - shift, 0) if shift else gf
-                gm = gm + cw_r[k : k + 1, cols] * moved[:length]
-                em = pltpu.roll(m, shift, 0) if shift else m
-                sums[k] = sums[k] + jnp.sum(gf[:length] * em[hw:], axis=0, keepdims=True)
-            gmb = gm.astype(BF)
-            parts.append(gmb)
-            gn[s] += dot_nt(gmb, wm[:, cols])
-        for k in range(window + 1):
-            small_put(SM_CONVW + k * (xbc // LN), b, sums[k])
-        return parts
-
-    def mixed_loop(b, _):
-        cols = ds(b * BW, BW)
-        for s, part in enumerate(mixed_body(b)):
-            nrm[s, :, cols] = part
-        return 0
-
-    service()
-    lax.fori_loop(0, 3, mixed_loop, 0)
-    service()
-    lax.fori_loop(3, 6, mixed_loop, 0)
-    service()
-    for s, part in enumerate(mixed_body(6)):
-        ggz[s, :, 0:BW] = part
     service()
     for s in range(seqs):
-        gn[s] += dot_nt(grl[s], ws3)
-    service()
+        for i in range(dm // BW):
+            cols = slice(i * BW, (i + 1) * BW)
+            pj = dot(nrm[s], wo[:, cols])
+            res_r[s, :, cols] = (tok[s, :, cols].astype(F32) + pj).astype(BF)
+        service()
+    res_copy = pltpu.make_async_copy(res_r, res_h, tok_sem.at[0])
+    res_copy.start()
+    for s in range(seqs):
+        for i in range(dm // BW):
+            cols = slice(i * BW, (i + 1) * BW)
+            gn[s, :, cols] = (
+                dot_nt(gy[s], wm[cols, :di])
+                + dot_nt(drv[s, :, 0:BW], wm[cols, di:])
+                + dot_nt(ggz[s], wg[cols, :])
+                + dot_nt(grl[s], ws3[cols])
+            )
+        service()
 
     @pl.when(has_next)
     def _():
@@ -1027,7 +1081,7 @@
         compiler_params=pltpu.CompilerParams(
             collective_id=0, has_side_effects=True, vmem_limit_bytes=65200 * 1024
         ),
-    )(*args)
+    )(*args[:4], ws.T, *args[5:])
     res, tg, g_out, g_gate, g_mixer, small = out
     gate0 = xbc // LN
     norm0 = gate0 + di // LN
@@ -1035,14 +1089,70 @@
     taps = conv_w.shape[0]
     heads0 = convw0 + taps * (xbc // LN)
     step0 = -(-(heads0 + 3) // 8) * 8
-    step = small[step0 : step0 + heads * (dm // LN)].reshape(dm // LN, heads, LN)
-    return (
-        res, tg, small[norm0:convw0].reshape(dm), g_gate.astype(F32), g_mixer.astype(F32),
-        step.transpose(0, 2, 1).reshape(dm, heads),
-        small[convw0:heads0].reshape(taps, xbc), small[:gate0].reshape(xbc),
-        small[heads0, :heads], small[heads0 + 1, :heads], small[heads0 + 2, :heads],
-        small[gate0:norm0].reshape(di), g_out.astype(F32),
-    )
+
+    def finish(res_i, tg_i, go_i, gw_i, gm_i, sm_i, *outs):
+        res_o, tg_o, ng_o, gw_o, gm_o, st_o, cw_o, cb_o, sb_o, lr_o, sk_o, gg_o, go_o = outs
+        res_o[...] = res_i[...]
+        tg_o[...] = tg_i[...]
+        go_o[...] = go_i[...].astype(F32)
+        gw_o[...] = gw_i[...].astype(F32)
+        gm_o[...] = gm_i[...].astype(F32)
+
+        @pl.when(pl.program_id(0) == 0)
+        def _():
+            for ref, first, count in (
+                (cb_o, 0, xbc // LN), (gg_o, gate0, di // LN), (ng_o, norm0, dm // LN),
+            ):
+                for i in range(count):
+                    ref[pl.ds(i * LN, LN)] = sm_i[first + i, :]
+            for k in range(taps):
+                for i in range(xbc // LN):
+                    r = convw0 + k * (xbc // LN) + i
+                    cw_o[k : k + 1, i * LN : (i + 1) * LN] = sm_i[r : r + 1, :]
+            for i, ref in enumerate((sb_o, lr_o, sk_o)):
+                ref[...] = sm_i[heads0 + i, 0:heads]
+            for i in range(dm // LN):
+                r = step0 + heads * i
+                st_o[:, i * LN : (i + 1) * LN] = sm_i[r : r + heads, :]
+
+    steps = 4
+
+    def rows_of(a, dim=0):
+        block = tuple(n // steps if i == dim else n for i, n in enumerate(a.shape))
+        return pl.BlockSpec(block, lambda t: tuple(t if i == dim else 0 for i in range(a.ndim)))
+
+    def whole(*shape):
+        return pl.BlockSpec(shape, lambda t: (0,) * len(shape))
+
+    def shape(*dims):
+        return jax.ShapeDtypeStruct(dims, F32)
+
+    small_shapes = {
+        2: (dm,), 5: (heads, dm), 6: (taps, xbc), 7: (xbc,), 8: (heads,), 9: (heads,),
+        10: (heads,), 11: (di,),
+    }
+    big_outs = {0: res, 1: tg, 3: g_gate, 4: g_mixer, 12: g_out}
+    final = pl.pallas_call(
+        finish,
+        grid=(steps,),
+        in_specs=[
+            rows_of(res, 1), rows_of(tg, 1), rows_of(g_out), rows_of(g_gate), rows_of(g_mixer),
+            whole(*small.shape),
+        ],
+        out_specs=[
+            rows_of(big_outs[i], 1 if i < 2 else 0) if i in big_outs else whole(*small_shapes[i])
+            for i in range(13)
+        ],
+        out_shape=[
+            jax.ShapeDtypeStruct(big_outs[i].shape, BF if i < 2 else F32)
+            if i in big_outs else shape(*small_shapes[i])
+            for i in range(13)
+        ],
+        compiler_params=pltpu.CompilerParams(vmem_limit_bytes=62 * 1024 * 1024),
+    )(res, tg, g_out, g_gate, g_mixer, small)
+    final = list(final)
+    final[5] = final[5].T
+    return tuple(final)
 
 
 def solution(mesh):

time: 168 us -> 155 us (0.923)
  other arithmetic: 10 us -> 0 us
  local copies, waits for them, and re-layouts: 7.65 us -> 0 us
  Pallas kernels: 150 us -> 154 us
    convert_element_type x3 -> x0, other arithmetic: 10 us -> none  [the longest x1 4.65 us: on_device(): g_gate.astype(F32)]
    pallas_call x0 -> x1, Pallas kernels: none -> 10 us  [on_device(): pl.pallas_call(finish, grid=(steps,), in_specs=[rows_of(res, 1), rows_of(...]
    pallas_call x1, Pallas kernels: 150 us -> 144 us  [on_device(): pl.pallas_call(functools.partial(layer_kernel, nctx), out_shape=(jax.Shap...]
    unnamed x14 -> x0, local copies, waits for them, and re-layouts: 4.01 us -> none
    reshape x5 -> x0, local copies, waits for them, and re-layouts: 3.12 us -> none  [the longest x1 1.27 us: on_device(): small[norm0:convw0].reshape(dm)]
where the time goes in v4:
time: 155 us; the launch traced here: 154 us
  Pallas kernels  154 us (99%)
    pallas_call x1, Pallas kernels, on_device(): pl.pallas_call(functools.partial(layer_kernel, nctx), out_shape=(jax.Shap...  144 us
    pallas_call x1, Pallas kernels, on_device(): pl.pallas_call(finish, grid=(steps,), in_specs=[rows_of(res, 1), rows_of(...  10 us

profile of v4, /device:TPU:0, one launch (start us, length us, event | category | flops | bytes accessed | tf_op | source)
XLA Modules:
  0.0 154.3 jit_solution(6272286925983973206)
XLA Ops:
  0.6 143.5 %shard_map.228 = (bf16[2,256,768]{2,1,0:T(8,128)(2,1)}, bf16[2,256,768]{2,1,0:T(8,128)(2,1)}, bf16[1536,768]{1,0:T(8,128)(2,1)}, bf16[768,1536]{1,0:T(8,128)(2,1...) custom-call(bf16[2,256,768]{2,1,0:T(8,128)(2,1)} %tok_h.1, f32[768]{0:T(1024)} %ng_r.1, bf16[768,1536]{1,0:T(8,128)(2,1)} %wg_h.1, ...), custom_call_target="tpu_custom_call" | custom-call | tf_op jit(solution)/shard_map/pallas_call | solution.py:1012
  144.2 10.0 %shard_map.229 = (bf16[2,256,768]{2,1,0:T(8,128)(2,1)}, bf16[2,256,768]{2,1,0:T(8,128)(2,1)}, f32[768]{0:T(1024)}, f32[768,1536]{1,0:T(8,128)}, f32[768,1792]{1,...) custom-call(bf16[2,256,768]{2,1,0:T(8,128)(2,1)} %get-tuple-element., ...), custom_call_target="tpu_custom_call" | custom-call | tf_op jit(solution)/shard_map/pallas_call | solution.py:1135

commit v5 on v4

--- a/solution.py
+++ b/solution.py
@@ -15,25 +15,29 @@
 LN = 128
 SKEW = 2
 PLAN = (
-    (1, 0, 2, 1, 0, 2, 3),
+    (0, 2, 3, 0, 2, 3, 1),
     (),
-    (1, 3),
+    (1,),
+    (),
     (0,),
     (),
+    (2,),
+    (3,),
+    (4, 0, 2, 1, 4),
+    (3,),
+    (0, 5, 4, 2, 1, 5),
+    (6, 3),
+    (6,),
+    (0, 4),
     (),
-    (2, 1),
-    (3, 0),
-    (4, 1, 3, 2, 4, 0),
-    (1,),
-    (4, 5, 1, 3),
-    (6, 5, 4, 2, 6, 0),
-    (1,),
     (),
-    (3, 1),
-    (5, 6),
-    (4, 0),
-    (2, 7, 6, 7, 5, 4, 7, 2, 0, 3, 7, 0, 6, 5, 4, 6, 7, 3, 7, 5, 4, 4, 7, 6, 5, 2, 2, 6, 6,
-    7, 7, 3, 5, 5),
+    (2, 5),
+    (6,),
+    (1, 0),
+    (),
+    (),
+    (7, 3, 7, 5, 4, 7, 3, 6, 1, 2, 5, 7, 4, 6, 1, 7, 5, 4, 6, 2, 2, 3, 3, 7, 5, 0, 0, 4, 1,
+    7, 6, 4, 5, 5, 7, 7, 6, 1, 6),
 )
 
 
@@ -739,6 +743,7 @@
 
     plan = list(PLAN)
     live = {}
+    slot_now = [seqs * nblk]
 
     def service(last=False):
         todo = [g for part in plan for g in part] if last else plan.pop(0)
@@ -746,11 +751,17 @@
             if g not in live:
                 live[g] = group_steps(*groups[g])
             next(live[g], None)
+            if slot_now[0] < b_slots:
+                backward_slot(slot_now[0])
+                slot_now[0] += 1
 
     for i in range(seqs * nblk // 2):
         s, i0 = (2 * i) // nblk, (2 * i) % nblk
 
-        def backward_body(b, _, s=s):
+        service()
+        slot0 = slot_now[0] - i0
+
+        def backward_body(b, _, s=s, slot0=slot0):
             made = [pair_backward(2 * b + h, s) for h in range(2)]
             t1, t2, t3 = (p + q for p, q in zip(made[0][1], made[1][1]))
             gsc[s, :half, :half] += t1
@@ -759,12 +770,13 @@
             for cols, _, lo, hi in made:
                 z[s, :half, cols] = lo
                 z[s, half:, cols] = hi
-            backward_slot((seqs + s) * nblk + b)
+            backward_slot(slot0 + b)
             return 0
 
-        service()
         lax.fori_loop(i0, i0 + 2, backward_body, 0)
-    slots_alone(backward_slot, 2 * seqs * nblk, b_slots)
+        slot_now[0] += 2
+    slots_alone(backward_slot, slot_now[0], b_slots)
+    slot_now[0] = b_slots
     service()
 
     ginf[...] = jnp.zeros_like(ginf)
@@ -960,7 +972,12 @@
             tok[s, rows, :] = (cot[s, rows, :].astype(F32) + back).astype(BF)
         return sums
 
-    n_sum = lax.fori_loop(0, length // 16, token_body, jnp.zeros((1, dm), F32))
+    n_sum = jnp.zeros((1, dm), F32)
+    for i in range(4):
+        n_sum = lax.fori_loop(
+            i * (length // 64), (i + 1) * (length // 64), token_body, n_sum, unroll=2
+        )
+        service()
     for i in range(dm // LN):
         small_one(SM_NORM + i, n_sum[:, i * LN : (i + 1) * LN])
     tg_copy = pltpu.make_async_copy(tok, tg_h, tok_sem.at[1])

time: 155 us -> 149 us (0.961)
  Pallas kernels: 154 us -> 148 us
    pallas_call x1, Pallas kernels: 144 us -> 138 us  [on_device(): pl.pallas_call(functools.partial(layer_kernel, nctx), out_shape=(jax.Shap...]
where the time goes in v5:
time: 149 us
  Pallas kernels  148 us (99%)
    pallas_call x1, Pallas kernels, on_device(): pl.pallas_call(functools.partial(layer_kernel, nctx), out_shape=(jax.Shap...  138 us
    pallas_call x1, Pallas kernels, on_device(): pl.pallas_call(finish, grid=(steps,), in_specs=[rows_of(res, 1), rows_of(...  10 us

profile of v5, /device:TPU:0, one launch (start us, length us, event | category | flops | bytes accessed | tf_op | source)
XLA Modules:
  0.0 148.8 jit_solution(6013721497370188482)
XLA Ops:
  0.6 137.9 %shard_map.228 = (bf16[2,256,768]{2,1,0:T(8,128)(2,1)}, bf16[2,256,768]{2,1,0:T(8,128)(2,1)}, bf16[1536,768]{1,0:T(8,128)(2,1)}, bf16[768,1536]{1,0:T(8,128)(2,1...) custom-call(bf16[2,256,768]{2,1,0:T(8,128)(2,1)} %tok_h.1, f32[768]{0:T(1024)} %ng_r.1, bf16[768,1536]{1,0:T(8,128)(2,1)} %wg_h.1, ...), custom_call_target="tpu_custom_call" | custom-call | tf_op jit(solution)/shard_map/pallas_call | solution.py:1029
  138.6 10.0 %shard_map.229 = (bf16[2,256,768]{2,1,0:T(8,128)(2,1)}, bf16[2,256,768]{2,1,0:T(8,128)(2,1)}, f32[768]{0:T(1024)}, f32[768,1536]{1,0:T(8,128)}, f32[768,1792]{1,...) custom-call(bf16[2,256,768]{2,1,0:T(8,128)(2,1)} %get-tuple-element., ...), custom_call_target="tpu_custom_call" | custom-call | tf_op jit(solution)/shard_map/pallas_call | solution.py:1152

commit v6 on v5

--- a/solution.py
+++ b/solution.py
@@ -37,7 +37,7 @@
     (),
     (),
     (7, 3, 7, 5, 4, 7, 3, 6, 1, 2, 5, 7, 4, 6, 1, 7, 5, 4, 6, 2, 2, 3, 3, 7, 5, 0, 0, 4, 1,
-    7, 6, 4, 5, 5, 7, 7, 6, 1, 6),
+    7, 6, 4, 5, 5, 6, 7, 7, 6, 1),
 )
 
 
@@ -92,7 +92,7 @@
     tok, cot, wg, wm, wo, halo, ne, nt, ext, fil, drv, scl, y, z, big, gy, ggz, nrm, nrt,
     acc_a, acc_b, gn, sum_s, in_f, out_b, in_b, sraw, st, cum, cum_t, pst, ptl, pdc,
     dlast, infl, outf, inf_t, outf_t, sco, sco_t, xx, tri, hs_d, hs_g, bdh,
-    res_r, tok_sem, skw, sm, sk_row_r, bufs, ar_s, ar_r, loc_sem, ex_s, ex_r,
+    res_r, tok_sem, sm, sk_row_r, bufs, ar_s, ar_r, loc_sem, ex_s, ex_r,
     in_sem, halo_s, halo_r, fs_s, fs_r, bs_s, bs_r, gh_s, gh_r,
 ):
     seqs, length, dm = tok.shape
@@ -160,8 +160,7 @@
     xx[...] = jnp.where((c_i >= first) & (c_i < first + hp) & (r_i < 96), 1.0, 0.0).astype(BF)
     t_r = lax.broadcasted_iota(jnp.int32, (length, length), 0)
     t_c = lax.broadcasted_iota(jnp.int32, (length, length), 1)
-    tri[0] = jnp.where(t_r >= t_c, 1.0, 0.0).astype(BF)
-    tri[1] = jnp.where(t_r <= t_c, 1.0, 0.0).astype(BF)
+    tri[...] = jnp.where(t_r >= t_c, 1.0, 0.0).astype(BF)
     k_i = lax.broadcasted_iota(jnp.int32, (heads, LN), 0)
     l_i = lax.broadcasted_iota(jnp.int32, (heads, LN), 1)
     rep = jnp.where((l_i % 32 == k_i) & (l_i < 96), 1.0, 0.0)
@@ -176,7 +175,7 @@
     bias3 = replicated(sb_r)
     rates3 = -jnp.exp(replicated(lr_r))
     sk8 = jnp.broadcast_to(replicated(sk_r), (8, LN))
-    skw[...] = dot(pieces3(sk8), xx[...])
+    sk_row_r[...] = dot(pieces3(sk8), xx[...])
 
     pl.semaphore_wait(
         barrier, has_prev.astype(jnp.int32) + has_next.astype(jnp.int32) + len(peers)
@@ -223,7 +222,7 @@
         sraw[s] = raw
         step = jax.nn.softplus(raw + bias3)
         st[s] = step
-        cu = dot3(tri[0], step * rates3)
+        cu = dot3(tri[...], step * rates3)
         cum[s] = cu
         cum_t[s] = cu.T
         last = cu[length - 1 : length]
@@ -232,12 +231,6 @@
         dec = jnp.exp(cu)
         pdc[s] = pieces3(dec)
         dlast[s] = dot(pieces3(dec[length - 8 :]), xx[...])
-
-    for s in range(seqs):
-        for b in range(dm // BW):
-            nt[b * BW : (b + 1) * BW, s * length : (s + 1) * length] = ne[
-                s, hw : hw + length, b * BW : (b + 1) * BW
-            ].T
 
     @pl.when(has_prev)
     def _():
@@ -270,8 +263,6 @@
         outf[s] = o_bf
         inf_t[s] = i_bf.T
         outf_t[s] = o_bf.T
-        sco[s] = dot_nt(o_bf, i_bf)
-        sco_t[s] = dot_nt(i_bf, o_bf)
 
     def forward_copy(q):
         return pltpu.make_async_remote_copy(
@@ -335,7 +326,7 @@
                 dr = sig * dot(pst[s], x)
                 sc = (dr * dot(ptl[s], x)).astype(BF)
                 made.append(
-                    (b, cols, m_bf, f, skw[0:1, cols] * sig, dr.astype(BF), sc, dot(inf_t[s], sc))
+                    (b, cols, m_bf, f, sk_row_r[7:8, cols] * sig, dr.astype(BF), sc, dot(inf_t[s], sc))
                 )
             for b, cols, m_bf, f, sk_sig, dr, sc, summ in made:
                 ext[s, :, cols] = m_bf
@@ -405,6 +396,16 @@
     loads[2].wait()
     loads[3].wait()
     loads[4].wait()
+
+    for s in range(seqs):
+        for b in range(dm // BW):
+            nt[b * BW : (b + 1) * BW, s * length : (s + 1) * length] = ne[
+                s, hw : hw + length, b * BW : (b + 1) * BW
+            ].T
+
+    for s in range(seqs):
+        sco[s] = dot_nt(outf[s], infl[s])
+        sco_t[s] = dot_nt(infl[s], outf[s])
 
     for s in range(seqs):
 
@@ -826,7 +827,7 @@
             gst = dot(infl[s], lt) * dot(ptl[s], x)
             gd = z[s, :, cols]
             gyf = gy[s, :, cols].astype(F32)
-            sk_row = skw[0:1, cols]
+            sk_row = sk_row_r[7:8, cols]
             gg = gst + gd
             ga = sk_row * gyf + stw * gg
             t1 = stw * sig * gst
@@ -914,7 +915,7 @@
     grl = []
     for s in range(seqs):
         gc = hs_d[s] + jnp.where(row_i == length - 1, bdh[s, 0:1], 0.0)
-        terms = dot3(tri[1], gc)
+        terms = dot3(jnp.where(t_r <= t_c, 1.0, 0.0).astype(BF), gc)
         gst = hs_g[s] + terms * rates3
         glr = glr + jnp.sum(terms * st[s], axis=0, keepdims=True)
         graw = gst * sigmoid(sraw[s] + bias3)
@@ -1080,13 +1081,12 @@
             vm((seqs, length, length), F32),
             vm((seqs, length, length), F32),
             vm((LN, di), BF),
-            vm((2, length, length), BF),
+            vm((length, length), BF),
             vm((seqs, length, LN), F32),
             vm((seqs, length, LN), F32),
             vm((seqs, 8, LN), F32),
             vm((seqs, length, dm), BF),
             dma((2,)),
-            vm((8, di), F32),
             vm((2, 128, LN), F32),
             vm((8, di), F32),
             bufs,
@@ -1096,7 +1096,7 @@
             dma((xbc // BW,)), dma((xbc // BW,)),
         ],
         compiler_params=pltpu.CompilerParams(
-            collective_id=0, has_side_effects=True, vmem_limit_bytes=65200 * 1024
+            collective_id=0, has_side_effects=True, vmem_limit_bytes=65400 * 1024
         ),
     )(*args[:4], ws.T, *args[5:])
     res, tg, g_out, g_gate, g_mixer, small = out

time: 149 us -> 148 us (level)
  no operation moved by 1% of the time
where the time goes in v6:
time: 148 us
  Pallas kernels  147 us (99%)
    pallas_call x1, Pallas kernels, on_device(): pl.pallas_call(functools.partial(layer_kernel, nctx), out_shape=(jax.Shap...  137 us
    pallas_call x1, Pallas kernels, on_device(): pl.pallas_call(finish, grid=(steps,), in_specs=[rows_of(res, 1), rows_of(...  10 us

profile of v6, /device:TPU:0, one launch (start us, length us, event | category | flops | bytes accessed | tf_op | source)
XLA Modules:
  0.0 147.5 jit_solution(17079906269631717577)
XLA Ops:
  0.6 136.7 %shard_map.228 = (bf16[2,256,768]{2,1,0:T(8,128)(2,1)}, bf16[2,256,768]{2,1,0:T(8,128)(2,1)}, bf16[1536,768]{1,0:T(8,128)(2,1)}, bf16[768,1536]{1,0:T(8,128)(2,1...) custom-call(bf16[2,256,768]{2,1,0:T(8,128)(2,1)} %tok_h.1, f32[768]{0:T(1024)} %ng_r.1, bf16[768,1536]{1,0:T(8,128)(2,1)} %wg_h.1, ...), custom_call_target="tpu_custom_call" | custom-call | tf_op jit(solution)/shard_map/pallas_call | solution.py:1030
  137.4 10.0 %shard_map.229 = (bf16[2,256,768]{2,1,0:T(8,128)(2,1)}, bf16[2,256,768]{2,1,0:T(8,128)(2,1)}, f32[768]{0:T(1024)}, f32[768,1536]{1,0:T(8,128)}, f32[768,1792]{1,...) custom-call(bf16[2,256,768]{2,1,0:T(8,128)(2,1)} %get-tuple-element., ...), custom_call_target="tpu_custom_call" | custom-call | tf_op jit(solution)/shard_map/pallas_call | solution.py:1152
